TPU v7x, 128 devices: a whole 4x4x4 slice. The times are simulated.
128 devices in a mesh: section: 4 (over x_lo, core), mp: 32 (over z, x_hi, y).
Axes of the slice: x: 4 (x_hi: 2, x_lo: 2; x = x_hi * 2 + x_lo), y: 4, z: 4, core: 2. Of those that a mesh axis runs over, the one named last changes fastest.
Arguments:
- tokens: bfloat16 [4, 256, 8192], P('section', 'mp'), may hold values from -6 to 6
- upstream: bfloat16 [4, 256, 8192], P('section', 'mp'), may hold values from -6 to 6
- norm_gain: float32 [4, 8192], P('section'), may hold values from 0.1 to 1.9
- w_query: bfloat16 [4, 8192, 8192], P('section', None, 'mp'), may hold values from -0.0625 to 0.0625
- w_output: bfloat16 [4, 8192, 8192], P('section', 'mp'), may hold values from -0.0625 to 0.0625
- w_keyvalue: bfloat16 [4, 7680, 2048], P('section', 'mp'), may hold values from -0.0625 to 0.0625
- image_feats: bfloat16 [512, 7680], P(('section', 'mp')), may hold values from -20 to 20
- visible: int32 [2], replicated, may hold values from 1 to 4, as said below
Outputs:
- grad_tokens: bfloat16 [4, 256, 8192], P('section', 'mp')
- grad_gain: float32 [4, 8192], P('section')
- grad_query: bfloat16 [4, 8192, 8192], P('section', None, 'mp')
- grad_output: bfloat16 [4, 8192, 8192], P('section', 'mp')
- grad_keyvalue: bfloat16 [4, 7680, 2048], P('section', 'mp')
- grad_image: float32 [512, 7680], P(('section', 'mp'))
Inputs may be any that keep to these rules, and one draw needn't show every extreme that they name: `visible`: never falls from block to block; the last block sees all 4 images.
All inputs are finite; a program needn't handle non-finite values.
Results may differ from a plain program's by a relative error of at most 0.014.
The roundings to bfloat16 on the way count: a program that leaves them out, or rounds other values in their place, can miss the bound.
Values may be sent and summed in bfloat16 or wider, within the bound.
A program may use at most 128 MiB of HBM per device.

v0:
```python
import jax
import jax.numpy as jnp
from jax import lax
from jax.sharding import PartitionSpec as P

HD = 128
GROUP = 8
HEADS_DEV = 2
BLOCK = 128
VROWS = 128


def fold_runs(stacked, device_count):
    runs = GROUP // HEADS_DEV
    kv_count = device_count // runs
    count = stacked.shape[0]
    shaped = stacked.reshape(count, kv_count, runs, 2, HD)
    summed = jnp.sum(shaped, axis=2, dtype=jnp.float32)
    return summed.transpose(0, 2, 1, 3).reshape(count, 2 * kv_count * HD).astype(jnp.bfloat16)


def per_device(tokens, upstream, norm_gain, w_query, w_output, w_keyvalue, image_feats, visible):
    mp_count = lax.axis_size("mp")
    section_count = lax.axis_size("section")
    x_local = tokens[0]
    cotangent_local = upstream[0]
    gain_row = norm_gain[0]
    w_q = w_query[0]
    w_o = w_output[0]
    w_kv = w_keyvalue[0]
    xfloat = x_local.astype(jnp.float32)
    rinv = lax.rsqrt(jnp.mean(xfloat * xfloat, axis=-1, keepdims=True) + 1e-05)
    normed_local = (xfloat * rinv * gain_row[None, :]).astype(jnp.bfloat16)
    normed, cotangent = (
        lax.all_gather(normed_local, "mp", axis=0, tiled=True),
        lax.all_gather(cotangent_local, "mp", axis=0, tiled=True),
    )
    wide_rows = lax.all_gather(image_feats, "section", axis=0, tiled=True)
    mixed = lax.all_to_all(wide_rows, "mp", split_axis=1, concat_axis=0, tiled=True)
    own_rows = image_feats.shape[0]
    feat_cols = mixed.reshape(mp_count, section_count, own_rows, mixed.shape[1])
    feat_cols = feat_cols.transpose(1, 0, 2, 3).reshape(
        mp_count * section_count * own_rows, mixed.shape[1]
    )
    feat_rows = feat_cols.shape[0]
    rows = feat_cols
    kv_share = lax.psum_scatter(
        jnp.dot(rows, w_kv, preferred_element_type=jnp.float32),
        "mp",
        scatter_dimension=0,
        tiled=True,
    )
    keyvalue = lax.all_gather(kv_share.astype(jnp.bfloat16), "mp", axis=0, tiled=True)
    index = lax.axis_index("mp")
    kv_head = index * HEADS_DEV // GROUP
    half_width = keyvalue.shape[1] // 2
    keys = lax.dynamic_slice_in_dim(keyvalue, kv_head * HD, HD, 1)
    values = lax.dynamic_slice_in_dim(keyvalue, half_width + kv_head * HD, HD, 1)
    tok_count = normed.shape[0]
    query = jnp.dot(normed, w_q, preferred_element_type=jnp.float32).astype(jnp.bfloat16)
    query = query.reshape(tok_count, HEADS_DEV, HD)
    scale = HD ** (-0.5)
    image_of = jnp.arange(feat_rows, dtype=jnp.int32) // VROWS
    seen = jnp.repeat(visible, BLOCK)
    allowed = image_of[None, :] < seen[:, None]
    scores = jnp.einsum("thd,rd->htr", query, keys, preferred_element_type=jnp.float32) * scale
    scores = jnp.where(allowed[None], scores, -1e30)
    top = jnp.max(scores, axis=-1, keepdims=True)
    expo = jnp.exp(scores - top)
    probs = expo / jnp.sum(expo, axis=-1, keepdims=True)
    weights = probs.astype(jnp.bfloat16)
    attn = jnp.einsum("htr,rd->thd", weights, values, preferred_element_type=jnp.float32)
    attn = attn.astype(jnp.bfloat16).reshape(tok_count, HEADS_DEV * HD)
    grad_out = jnp.einsum("ta,td->ad", attn, cotangent, preferred_element_type=jnp.float32).astype(
        jnp.bfloat16
    )
    d_attn = jnp.einsum("td,ad->ta", cotangent, w_o, preferred_element_type=jnp.float32).astype(
        jnp.bfloat16
    )
    d_attn = d_attn.reshape(tok_count, HEADS_DEV, HD)
    d_prob = jnp.einsum("thd,rd->htr", d_attn, values, preferred_element_type=jnp.float32)
    d_value = jnp.einsum("htr,thd->rd", weights, d_attn, preferred_element_type=jnp.float32).astype(
        jnp.bfloat16
    )
    delta = jnp.sum(probs * d_prob, axis=-1, keepdims=True)
    d_score = (probs * (d_prob - delta) * scale).astype(jnp.bfloat16)
    d_query = jnp.einsum("htr,rd->thd", d_score, keys, preferred_element_type=jnp.float32).astype(
        jnp.bfloat16
    )
    d_query = d_query.reshape(tok_count, HEADS_DEV * HD)
    d_key = jnp.einsum("htr,thd->rd", d_score, query, preferred_element_type=jnp.float32).astype(
        jnp.bfloat16
    )
    pair_terms = jnp.concatenate([d_key, d_value], axis=1)
    stacked = lax.all_gather(pair_terms, "mp", axis=1, tiled=True)
    d_keyvalue = fold_runs(stacked, mp_count)
    grad_q = jnp.einsum("td,ta->da", normed, d_query, preferred_element_type=jnp.float32).astype(
        jnp.bfloat16
    )
    grad_kv = jnp.einsum(
        "rv,rc->vc", feat_cols, d_keyvalue, preferred_element_type=jnp.float32
    ).astype(jnp.bfloat16)
    d_feats = jnp.einsum("rc,vc->rv", d_keyvalue, w_kv, preferred_element_type=jnp.float32)
    rows = d_query
    d_normed = lax.psum_scatter(
        jnp.einsum("ta,da->td", rows, w_q, preferred_element_type=jnp.float32),
        "mp",
        scatter_dimension=0,
        tiled=True,
    )
    scaled = d_normed * gain_row[None, :]
    gain_part = jnp.sum(d_normed * xfloat * rinv, axis=0)
    grad_x = rinv * scaled - xfloat * rinv * rinv * rinv * jnp.mean(
        xfloat * scaled, axis=-1, keepdims=True
    )
    grad_g = lax.psum(gain_part, "mp")
    summed = lax.psum_scatter(d_feats, "section", scatter_dimension=0, tiled=True)
    grad_image = lax.all_to_all(summed, "mp", split_axis=0, concat_axis=1, tiled=True)
    return (
        grad_x.astype(jnp.bfloat16)[None],
        grad_g[None],
        grad_q[None],
        grad_out[None],
        grad_kv[None],
        grad_image,
    )


def solution(mesh):
    placed = (
        P("section", "mp", None),
        P("section", "mp", None),
        P("section", None),
        P("section", None, "mp"),
        P("section", "mp", None),
        P("section", "mp", None),
        P(("section", "mp"), None),
        P(),
    )
    return jax.shard_map(
        per_device,
        mesh=mesh,
        in_specs=placed,
        out_specs=(
            P("section", "mp", None),
            P("section", None),
            P("section", None, "mp"),
            P("section", "mp", None),
            P("section", "mp", None),
            P(("section", "mp"), None),
        ),
        check_vma=False,
    )
```

profile of v0, /device:TPU:0, one launch (start us, length us, event | category | flops | bytes accessed | tf_op | source)
XLA Modules:
  0.0 994.1 jit_solution(10382591681003636224)
XLA Ops:
  7.2 6.1 all-gather.1
  13.3 0.6 all_to_all.26
  13.9 0.2 copy.43
  14.1 21.8 %all_to_all.35 = bf16[16,32,240]{2,0,1:T(8,128)(2,1)S(1)} all-to-all(bf16[16,32,240]{2,0,1:T(8,128)(2,1)S(1)} %copy.43), channel_id=1, replica_groups=mesh['section'=4,'mp'=32] {'mp'}, dimensions={1} | all-to-all | bytes 491520 | tf_op jit(solution)/shard_map/all_to_all | solution.py:39
  35.9 0.1 copy.44
  36.0 0.2 copy.45
  36.2 0.2 reshape.103
  36.4 2.7 fusion.37
  39.2 0.0 all-gather.9.cloned.1.call-start
  39.2 0.2 fusion.48
  39.4 0.8 fusion.43
  40.2 0.7 all-gather.13.cloned.1.call-update
  41.0 186.3 %reduce-scatter.4.cloned.1.call-done = f32[16,2048]{1,0:T(8,128)} async-done(((f32[512,2048]{1,0:T(8,128)}), f32[16,2048]{1,0:T(8,128)}) %reduce-scatter.4.cloned.1.call-update) | async-done | bytes 131088 | tf_op jit(solution)/shard_map/reduce_scatter | solution.py:47
  227.3 1.5 convert_element_type.75
  228.9 0.0 all-gather.11.cloned.1.call-start
  229.0 0.1 broadcast_bitcast_fusion
  229.0 0.1 broadcast_compare_fusion
  229.2 77.0 %all-gather.9.cloned.1.call-done = bf16[256,8192]{1,0:T(8,128)(2,1)} async-done(((bf16[8,8192]{1,0:T(8,128)(2,1)}), bf16[256,8192]{1,0:T(8,128)(2,1)}) %all-gather.9.cloned.1.call-update) | async-done | bytes 4194320 | tf_op jit(solution)/shard_map/all_gather | solution.py:35
  306.2 5.2 fusion.23
  311.4 77.2 %all-gather.13.cloned.1.call-done = bf16[1,256,8192]{2,1,0:T(8,128)(2,1)} async-done(((bf16[1,8,8192]{2,1,0:T(8,128)(2,1)}), bf16[1,256,8192]{2,1,0:T(8,128)(2,1)}) %all-gather.13.cloned.1.call-update) | async-done | bytes 4194320 | tf_op jit(solution)/shard_map/all_gather | solution.py:36
  388.6 4.7 fusion.26
  393.3 68.4 %all-gather.7.cloned.1.call-done = bf16[512,2048]{1,0:T(8,128)(2,1)} async-done(((bf16[16,2048]{1,0:T(8,128)(2,1)}), bf16[512,2048]{1,0:T(8,128)(2,1)}) %all-gather.7.cloned.1.call-update) | async-done | bytes 2097168 | tf_op jit(solution)/shard_map/all_gather | solution.py:53
  461.8 1.2 convolution_bitcast_fusion
  462.9 2.3 fusion.91
  465.3 2.0 fusion.21
  467.3 1.6 fusion.22
  469.0 0.7 pad_maximum_fusion
  469.7 0.0 reduce-scatter.6.cloned.1.call-start
  469.8 2.1 convolution_convert_fusion.4
  471.8 6.8 fusion.8
  478.6 0.2 reduce-scatter.8.cloned.1.call-start
  478.9 2.4 convolution_convert_fusion.3
  481.2 90.7 %all-gather.11.cloned.1.call-done = bf16[512,8192]{0,1:T(8,128)(2,1)} async-done(((bf16[512,256]{0,1:T(8,128)(2,1)}), bf16[512,8192]{0,1:T(8,128)(2,1)}) %all-gather.11.cloned.1.call-update) | async-done | bytes 8388624 | tf_op jit(solution)/shard_map/all_gather | solution.py:95
  572.0 7.1 reduce
  579.1 1.8 copy.54
  580.9 1.5 fusion.35
  582.4 5.7 fusion.3
  588.1 3.3 fusion.2
  591.4 1.7 fusion.12
  593.1 181.7 %reduce-scatter.6.cloned.1.call-done = f32[8,8192]{1,0:T(8,128)} async-done(((f32[256,8192]{1,0:T(8,128)}), f32[8,8192]{1,0:T(8,128)}) %reduce-scatter.6.cloned.1.call-update) | async-done | bytes 262160 | tf_op jit(solution)/shard_map/reduce_scatter | solution.py:105
  774.9 1.2 fusion.51
  776.1 14.0 %reduce-scatter.8.cloned.1.call-done = f32[128,240]{0,1:T(8,128)} async-done(((f32[512,240]{0,1:T(8,128)}), f32[128,240]{0,1:T(8,128)}) %reduce-scatter.8.cloned.1.call-update) | async-done | bytes 122896 | tf_op jit(solution)/shard_map/reduce_scatter | solution.py:117
  790.1 1.0 copy.55
  791.1 0.7 all_to_all.29
  791.8 9.2 all-to-all-start.1
  801.0 1.7 fusion.54
  802.8 183.7 %psum.7 = f32[1,8192]{1,0:T(1,128)} all-reduce(f32[1,8192]{1,0:T(1,128)S(1)} %bitcast.148), channel_id=1, replica_groups=mesh['section'=4,'mp'=32] {'mp'}, use_global_device_ids=true, to_apply=%region_8.9 | all-reduce | flops 8192 | bytes 65536 | tf_op jit(solution)/shard_map/psum | solution.py:116
  986.5 0.8 all_to_all.32
  (28 shorter events, 0.3 us)
Async XLA Ops:
  7.2 29.2 %copy-start = (bf16[1,240,2048]{2,1,0:T(8,128)(2,1)S(1)}, bf16[1,240,2048]{2,1,0:T(8,128)(2,1)}, u32[]{:S(2)}) copy-start(bf16[1,240,2048]{2,1,0:T(8,128)(2,1)} %param.13) | copy-start | bytes 2949124
  7.2 220.1 %reduce-scatter.4.cloned.1.call-start = ((), (), s32[]{:S(2)}) async-start(), calls=%async_computation.5 | async-start | bytes 4325376 | tf_op jit(solution)/shard_map/reduce_scatter | solution.py:47
  36.4 2.8 copy-start.2
  36.4 3.0 copy-start.5
  39.1 189.8 %copy-start.6 = (s32[2]{0:T(128)S(1)}, s32[2]{0:T(128)}, u32[]{:S(2)}) copy-start(s32[2]{0:T(128)} %param.15) | copy-start | bytes 28
  39.2 267.0 %all-gather.9.cloned.1.call-start = ((), (), s32[]{:S(2)}) async-start(), calls=%async_computation.7 | async-start | bytes 4325376 | tf_op jit(solution)/shard_map/all_gather | solution.py:35
  40.2 348.4 %all-gather.13.cloned.1.call-start = ((), (), s32[]{:S(2)}) async-start(), calls=%async_computation.11 | async-start | bytes 4325376 | tf_op jit(solution)/shard_map/all_gather | solution.py:36
  40.9 420.8 %all-gather.7.cloned.1.call-start = ((), (), s32[]{:S(2)}) async-start(), calls=%async_computation.6 | async-start | bytes 2162688 | tf_op jit(solution)/shard_map/all_gather | solution.py:53
  228.9 343.1 %all-gather.11.cloned.1.call-start = ((), (), s32[]{:S(2)}) async-start(), calls=%async_computation.9 | async-start | bytes 8650752 | tf_op jit(solution)/shard_map/all_gather | solution.py:95
  469.7 305.1 %reduce-scatter.6.cloned.1.call-start = ((), (), s32[]{:S(2)}) async-start(), calls=%async_computation.8 | async-start | bytes 8650752 | tf_op jit(solution)/shard_map/reduce_scatter | solution.py:105
  471.8 6.8 copy-start.3
  478.6 311.5 %reduce-scatter.8.cloned.1.call-start = ((), (), s32[]{:S(2)}) async-start(), calls=%async_computation.10 | async-start | bytes 614400 | tf_op jit(solution)/shard_map/reduce_scatter | solution.py:117
  582.4 5.7 copy-start.1
  582.4 5.7 copy-start.4
  791.8 194.7 %all-to-all-start.1 = ((f32[32,4,240]{2,1,0:T(4,128)}), f32[32,4,240]{2,1,0:T(4,128)S(1)}, u32[]{:S(2)}, u32[]{:S(2)}) async-start(f32[32,4,240]{2,1,0:T(4,128)} %all_to_all.29), calls=%async_computation.4 | async-start | bytes 262144 | tf_op jit(solution)/shard_map/all_to_all | solution.py:118
Sparse Core Ops, SparseCore 0:
  39.3 187.9 reduce-scatter.3
  230.9 75.2 all-gather.8
  309.3 79.2 all-gather.12
  392.2 69.5 all-gather.6
  469.8 102.0 all-gather.10
  574.2 200.5 reduce-scatter.5
  777.3 12.8 reduce-scatter.7
where the time goes:
time: 995 us; the launch traced here: 994 us
  waiting for transfers between devices  696 us (70%)
  blocking collectives  212 us (21%)
  matrix products  43.3 us (4%)
  between operations  14.4 us (1%)
  other arithmetic  13.4 us (1%)
    reduce_scatter x1, waiting for transfers between devices, per_device(): lax.psum_scatter(jnp.dot(rows, w_kv, preferred_element_type=jnp.float32),...  186 us
    psum x1, blocking collectives, per_device(): grad_g = lax.psum(gain_part, 'mp')  184 us
    reduce_scatter x1, waiting for transfers between devices, per_device(): lax.psum_scatter(jnp.einsum('ta,da->td', rows, w_q, preferred_element_typ...  182 us
    all_gather x1, waiting for transfers between devices, per_device(): stacked = lax.all_gather(pair_terms, 'mp', axis=1, tiled=True)  90.7 us
    all_gather x1, waiting for transfers between devices, per_device(): lax.all_gather(cotangent_local, 'mp', axis=0, tiled=True)  77.2 us
    all_gather x1, waiting for transfers between devices, per_device(): lax.all_gather(normed_local, 'mp', axis=0, tiled=True)  77 us
    all_gather x1, waiting for transfers between devices, per_device(): lax.all_gather(kv_share.astype(jnp.bfloat16), 'mp', axis=0, tiled=True)  68.4 us
    all_to_all x1, blocking collectives, per_device(): lax.all_to_all(wide_rows, 'mp', split_axis=1, concat_axis=0, tiled=True)  21.8 us
  transfers between devices with their start and end apart: 8, of which 7 were waited for; matrix products, arithmetic and copies ran while one was open for 5% of the time, Pallas kernels for 0%

commit v1 on v0

v1 whole, which is shorter than its diff:
```python
import jax
import jax.numpy as jnp
from jax import lax
from jax.experimental import pallas as pl
from jax.experimental.pallas import tpu as pltpu
from jax.sharding import PartitionSpec as P

MESH = pl.DeviceIdType.MESH
F32 = jnp.float32
BF16 = jnp.bfloat16
TOK = 256
D = 8192
HALF = D // 2
CHUNK = 1024
HD = 128
VCOLS = 240
SCALE = HD ** (-0.5)
NSEM = 96

NT = (((1,), (1,)), ((), ()))
TN = (((0,), (0,)), ((), ()))


def dot(a, b, dims=(((1,), (0,)), ((), ()))):
    return lax.dot_general(a, b, dims, preferred_element_type=F32)


class Links:
    def __init__(self, send_sems, recv_sems):
        self.s = lax.axis_index("section")
        index = lax.axis_index("mp")
        self.z, self.x, self.y = index // 8, (index // 4) % 2, index % 4
        self.send_sems, self.recv_sems = send_sems, recv_sems
        self.copies = []

    def coord(self, axis, d):
        if axis == "x":
            return (self.x + d) % 2
        return (getattr(self, axis) + d) % 4

    def peer(self, axis, d):
        at = {"s": self.s, "z": self.z, "x": self.x, "y": self.y}
        at[axis] = self.coord(axis, d)
        return (at["s"], at["z"] * 8 + at["x"] * 4 + at["y"])

    def barrier(self):
        sem = pltpu.get_barrier_semaphore()
        peers = [(a, d) for a in ("z", "y", "s") for d in (1, 2, 3)] + [("x", 1)]
        for a, d in peers:
            pl.semaphore_signal(sem, inc=1, device_id=self.peer(a, d), device_id_type=MESH)
        pl.semaphore_wait(sem, len(peers))

    def send(self, axis, d, src, dst):
        at = len(self.copies)
        copy = pltpu.make_async_remote_copy(
            src_ref=src,
            dst_ref=dst,
            send_sem=self.send_sems.at[at],
            recv_sem=self.recv_sems.at[at],
            device_id=self.peer(axis, d),
            device_id_type=MESH,
        )
        copy.start()
        self.copies.append(copy)
        return copy

    def ring(self, axis, src, dst):
        return [self.send(axis, d, src(d), dst(d)) for d in (1, 3, 2)]

    def finish(self):
        for copy in self.copies:
            copy.wait_send()


def arrive(copies):
    for copy in copies:
        copy.wait_recv()


def columns(start, stop, body, step=CHUNK):
    @pl.loop(0, (stop - start) // step)
    def _(i):
        body(pl.ds(pl.multiple_of(start + i * step, step), step))


def layer_kernel(
    tok_ref, cot_ref, gain_ref, vis_ref, feat_ref, wq_hbm, wo_hbm, wkv_hbm,
    n_out, c_out, attn_out, dq_out, gkv_out, gx_out, gg_out, gi_out,
    n_all, c_all, wq, wo, wkv,
    fold_n, fold_c, from_n, from_c,
    pk, pv, k1, v1, ks1, vs1, k2, v2, ks2, vs2, kx, vx, keys, values,
    dk, dv, rk, rv, dkg, dvg,
    pd, da1, db1, sa1, sb1, da2, db2, own_d, fold_d, from_d,
    df, dfr, img_s, img_z, img_x, gz, gy, gx2,
    send_sems, recv_sems, local_sems,
):
    net = Links(send_sems, recv_sems)
    s, z, x, y = net.s, net.z, net.x, net.y
    loads = []
    wkv[VCOLS:, :] = jnp.zeros((256 - VCOLS, 2048), BF16)
    for i, (src, dst) in enumerate(((wkv_hbm, wkv.at[:VCOLS]), (wq_hbm, wq), (wo_hbm, wo))):
        copy = pltpu.make_async_copy(src, dst, local_sems.at[i])
        copy.start()
        loads.append(copy)
    net.barrier()

    xf = tok_ref[...].astype(F32)
    rinv = lax.rsqrt(jnp.mean(xf * xf, axis=-1, keepdims=True) + 1e-05)

    def normed_at(cols):
        return tok_ref[:, cols].astype(F32) * rinv * gain_ref[:, cols]

    def fold_step(i):
        lo = pl.ds(pl.multiple_of(i * CHUNK, CHUNK), CHUNK)
        hi = pl.ds(pl.multiple_of(HALF + i * CHUNK, CHUNK), CHUNK)
        fold_n[:, lo] = jnp.concatenate([normed_at(lo), normed_at(hi)], axis=0).astype(BF16)
        fold_c[:, lo] = jnp.concatenate(
            [cot_ref[:, lo].astype(F32), cot_ref[:, hi].astype(F32)], axis=0
        ).astype(BF16)

    pl.loop(0, HALF // CHUNK)(fold_step)
    x_n = net.send("x", 1, fold_n, from_n)
    x_c = net.send("x", 1, fold_c, from_c)

    loads[0].wait()

    def kv_step(h):
        cols = pl.ds(pl.multiple_of(h * HD, HD), HD)
        vcols = pl.ds(pl.multiple_of(1024 + h * HD, HD), HD)
        feats = feat_ref[...]
        pk[h // 2, h % 2] = dot(feats, wkv[:, cols]).reshape(4, 128, HD)
        pv[h // 2, h % 2] = dot(feats, wkv[:, vcols]).astype(BF16).reshape(4, 128, HD)

    pl.loop(0, 8)(kv_step)
    k_1 = net.ring("y", lambda d: pk.at[:, :, net.coord("y", d)], lambda d: k1.at[d - 1])
    v_1 = net.ring("z", lambda d: pv.at[net.coord("z", d)], lambda d: v1.at[d - 1])

    def unfold(folded, received, full):
        def step(i):
            lo = pl.ds(pl.multiple_of(i * CHUNK, CHUNK), CHUNK)
            hi = pl.ds(pl.multiple_of(HALF + i * CHUNK, CHUNK), CHUNK)
            mine = folded[:, lo].astype(F32)
            other = received[:, lo].astype(F32)
            for at, cols in ((0, lo), (8, hi)):
                a, b = mine[at : at + 8], other[at : at + 8]
                first = jnp.where(x == 0, a, b)
                second = jnp.where(x == 0, b, a)
                full[z, y, :, cols] = jnp.concatenate([first, second], axis=0).astype(BF16)

        pl.loop(0, HALF // CHUNK)(step)

    a_cols, b_cols = pl.ds(0, HALF), pl.ds(HALF, HALF)

    def gather_start(full):
        own_a, own_b = full.at[z, y, :, a_cols], full.at[z, y, :, b_cols]
        za = net.ring("z", lambda d: own_a, lambda d: own_a)
        yb = net.ring("y", lambda d: own_b, lambda d: own_b)
        return za, yb

    def gather_on(full, za, yb):
        arrive(za)
        part = full.at[:, y, :, a_cols]
        out = net.ring("y", lambda d: part, lambda d: part)
        arrive(yb)
        part_b = full.at[z, :, :, b_cols]
        return out + net.ring("z", lambda d: part_b, lambda d: part_b)

    x_n.wait_recv()
    unfold(fold_n, from_n, n_all)
    n_1 = gather_start(n_all)

    arrive(k_1)
    for a in range(4):
        for b in range(2):
            total = pk[a, b, y]
            for d in range(3):
                total += k1[d, a, b]
            ks1[a, b] = total
    k_2 = net.ring("z", lambda d: ks1.at[net.coord("z", d)], lambda d: k2.at[d - 1])
    arrive(v_1)
    for b in range(2):
        for c in range(4):
            total = pv[z, b, c].astype(F32)
            for d in range(3):
                total += v1[d, b, c].astype(F32)
            vs1[b, c] = total.astype(BF16)
    v_2 = net.ring("y", lambda d: vs1.at[:, net.coord("y", d)], lambda d: v2.at[d - 1])

    n_2 = gather_on(n_all, *n_1)
    x_c.wait_recv()
    unfold(fold_c, from_c, c_all)

    arrive(k_2)
    arrive(v_2)
    for b in range(2):
        total = ks1[z, b]
        vtotal = vs1[b, y].astype(F32)
        for d in range(3):
            total += k2[d, b]
            vtotal += v2[d, b].astype(F32)
        ks2[b] = total
        vs2[b] = vtotal.astype(BF16)
    k_x = net.send("x", 1, ks2.at[1 - x], kx)
    v_x = net.send("x", 1, vs2.at[1 - x], vx)
    c_1 = gather_start(c_all)
    k_x.wait_recv()
    v_x.wait_recv()
    keys[y] = (ks2[x] + kx[...]).astype(BF16)
    values[y] = (vs2[x].astype(F32) + vx[...].astype(F32)).astype(BF16)
    k_3 = net.ring("y", lambda d: keys.at[y], lambda d: keys.at[y])
    v_3 = net.ring("y", lambda d: values.at[y], lambda d: values.at[y])

    arrive(n_2)
    stores = []
    copy = pltpu.make_async_copy(n_all, n_out, local_sems.at[3])
    copy.start()
    stores.append(copy)
    c_2 = gather_on(c_all, *c_1)

    loads[1].wait()

    def query_step(i, acc):
        cols = pl.ds(pl.multiple_of(i * CHUNK, CHUNK), CHUNK)
        return acc + dot(n_all[:, :, :, cols].reshape(TOK, CHUNK), wq[cols, :])

    query = lax.fori_loop(0, D // CHUNK, query_step, jnp.zeros((TOK, 256), F32)).astype(BF16)

    arrive(k_3)
    arrive(v_3)
    key = keys[...].reshape(512, HD)
    value = values[...].reshape(512, HD)
    image_of = lax.broadcasted_iota(jnp.int32, (TOK, 512), 1) // 128
    late = lax.broadcasted_iota(jnp.int32, (TOK, 512), 0) >= 128
    allowed = image_of < jnp.where(late, vis_ref[1], vis_ref[0])
    probs, weights = [], []
    for j in range(2):
        q = query[:, j * HD : (j + 1) * HD]
        scores = jnp.where(allowed, dot(q, key, NT) * SCALE, -1e30)
        expo = jnp.exp(scores - jnp.max(scores, axis=-1, keepdims=True))
        prob = expo / jnp.sum(expo, axis=-1, keepdims=True)
        probs.append(prob)
        weights.append(prob.astype(BF16))
        attn_out[:, j * HD : (j + 1) * HD] = dot(weights[j], value).astype(BF16)

    arrive(c_2)
    copy = pltpu.make_async_copy(c_all, c_out, local_sems.at[4])
    copy.start()
    stores.append(copy)
    loads[2].wait()

    def d_attn_step(i, acc):
        cols = pl.ds(pl.multiple_of(i * CHUNK, CHUNK), CHUNK)
        return acc + dot(c_all[:, :, :, cols].reshape(TOK, CHUNK), wo[:, cols], NT)

    d_attn = lax.fori_loop(0, D // CHUNK, d_attn_step, jnp.zeros((TOK, 256), F32)).astype(BF16)
    d_key = jnp.zeros((512, HD), F32)
    d_value = jnp.zeros((512, HD), F32)
    for j in range(2):
        heads = slice(j * HD, (j + 1) * HD)
        da = d_attn[:, heads]
        d_prob = dot(da, value, NT)
        delta = jnp.sum(probs[j] * d_prob, axis=-1, keepdims=True)
        d_score = (probs[j] * (d_prob - delta) * SCALE).astype(BF16)
        dq_out[:, heads] = dot(d_score, key).astype(BF16)
        d_key += dot(d_score, query[:, heads], TN)
        d_value += dot(weights[j], da, TN)
    dk[...] = d_key.astype(BF16).reshape(4, 128, HD)
    dv[...] = d_value.astype(BF16).reshape(4, 128, HD)
    dk_1 = net.ring("y", lambda d: dk.at[net.coord("y", d)], lambda d: rk.at[d - 1])
    dv_1 = net.ring("y", lambda d: dv.at[net.coord("y", d)], lambda d: rv.at[d - 1])

    def d_normed_step(cols):
        part = dot(dq_out[...], wq[cols, :], NT)
        pd[:, :, :, cols] = part.astype(BF16).reshape(4, 4, 16, CHUNK)

    columns(0, HALF, d_normed_step)
    da_1 = net.ring(
        "y", lambda d: pd.at[:, net.coord("y", d), :, a_cols], lambda d: da1.at[d - 1]
    )
    columns(HALF, D, d_normed_step)
    db_1 = net.ring("z", lambda d: pd.at[net.coord("z", d), :, :, b_cols], lambda d: db1.at[d - 1])

    arrive(dk_1)
    arrive(dv_1)
    total = dk[y].astype(F32)
    vtotal = dv[y].astype(F32)
    for d in range(3):
        total += rk[d].astype(F32)
        vtotal += rv[d].astype(F32)
    dkg[z, x, y] = total.astype(BF16)
    dvg[z, x, y] = vtotal.astype(BF16)
    mine_k, mine_v = dkg.at[z, x, y], dvg.at[z, x, y]
    dk_2 = net.send("x", 1, mine_k, mine_k)
    dv_2 = net.send("x", 1, mine_v, mine_v)
    dk_2.wait_recv()
    dv_2.wait_recv()
    pair_k, pair_v = dkg.at[z, :, y], dvg.at[z, :, y]
    dk_3 = net.ring("z", lambda d: pair_k, lambda d: pair_k)
    dv_3 = net.ring("y", lambda d: pair_v, lambda d: pair_v)
    arrive(dk_3)
    line_k = dkg.at[:, :, y]
    dk_4 = net.ring("y", lambda d: line_k, lambda d: line_k)
    arrive(dv_3)
    line_v = dvg.at[z]
    dv_4 = net.ring("z", lambda d: line_v, lambda d: line_v)

    arrive(da_1)

    def sum_a(i):
        cols = pl.ds(pl.multiple_of(i * CHUNK, CHUNK), CHUNK)
        total = pd[:, y, :, cols].astype(F32)
        for d in range(3):
            total += da1[d, :, :, cols].astype(F32)
        sa1[:, :, cols] = total.astype(BF16)

    pl.loop(0, HALF // CHUNK)(sum_a)
    da_2 = net.ring("z", lambda d: sa1.at[net.coord("z", d)], lambda d: da2.at[d - 1])
    arrive(db_1)

    def sum_b(i):
        cols = pl.ds(pl.multiple_of(i * CHUNK, CHUNK), CHUNK)
        far = pl.ds(pl.multiple_of(HALF + i * CHUNK, CHUNK), CHUNK)
        total = pd[z, :, :, far].astype(F32)
        for d in range(3):
            total += db1[d, :, :, cols].astype(F32)
        sb1[:, :, cols] = total.astype(BF16)

    pl.loop(0, HALF // CHUNK)(sum_b)
    db_2 = net.ring("y", lambda d: sb1.at[net.coord("y", d)], lambda d: db2.at[d - 1])

    arrive(dk_4)
    arrive(dv_4)
    feats = feat_ref[...]
    d_feats = jnp.zeros((512, 256), F32)
    for h in range(8):
        for at, full in ((h * HD, dkg), (1024 + h * HD, dvg)):
            grad = full[h // 2, h % 2].reshape(512, HD)
            gkv_out[:, at : at + HD] = dot(feats, grad, TN).astype(BF16)
            d_feats += dot(grad, wkv[:, at : at + HD], NT)
    df[...] = d_feats.reshape(4, 128, 256)
    f_1 = net.ring("s", lambda d: df.at[net.coord("s", d)], lambda d: dfr.at[d - 1])

    arrive(da_2)
    arrive(db_2)

    def sum_ab(i):
        cols = pl.ds(pl.multiple_of(i * CHUNK, CHUNK), CHUNK)
        ta = sa1[z, :, cols].astype(F32)
        tb = sb1[y, :, cols].astype(F32)
        for d in range(3):
            ta += da2[d, :, cols].astype(F32)
            tb += db2[d, :, cols].astype(F32)
        own_d[:8, cols] = jnp.where(x == 0, ta[:8], ta[8:])
        own_d[8:, cols] = jnp.where(x == 0, tb[:8], tb[8:])
        fold_d[:, cols] = jnp.concatenate(
            [jnp.where(x == 0, ta[8:], ta[:8]), jnp.where(x == 0, tb[8:], tb[:8])], axis=0
        ).astype(BF16)

    pl.loop(0, HALF // CHUNK)(sum_ab)
    d_x = net.send("x", 1, fold_d, from_d)

    arrive(f_1)
    img = df[s]
    for d in range(3):
        img += dfr[d]
    img_s[...] = img.reshape(4, 32, 256)
    img_z[z] = img_s[z]
    f_2 = net.ring("z", lambda d: img_s.at[net.coord("z", d)], lambda d: img_z.at[z])

    d_x.wait_recv()
    both = own_d[...] + from_d[...].astype(F32)
    dn = jnp.concatenate([both[:8], both[8:]], axis=1)
    xf = tok_ref[...].astype(F32)
    scaled = dn * gain_ref[...]
    gx_out[...] = (
        rinv * scaled - xf * rinv * rinv * rinv * jnp.mean(xf * scaled, axis=-1, keepdims=True)
    ).astype(BF16)
    gain = jnp.sum(dn * xf * rinv, axis=0, keepdims=True)
    for i in range(8):
        gz[z, i : i + 1, :] = gain[:, i * 1024 : (i + 1) * 1024]
    g_1 = net.ring("z", lambda d: gz.at[z], lambda d: gz.at[z])

    arrive(f_2)
    img_x[x] = img_z[:, pl.ds(pl.multiple_of(x * 16, 16), 16), :]
    far = pl.ds(pl.multiple_of((1 - x) * 16, 16), 16)
    f_3 = net.send("x", 1, img_z.at[:, far], img_x.at[x])
    arrive(g_1)
    gy[y] = (gz[0] + gz[1]) + (gz[2] + gz[3])
    g_2 = net.ring("y", lambda d: gy.at[y], lambda d: gy.at[y])
    f_3.wait_recv()

    def tile(d):
        return pl.ds(pl.multiple_of((net.coord("y", d) // 2) * 8, 8), 8)

    gi_out[y] = img_x[:, :, tile(0), :]
    f_4 = net.ring("y", lambda d: img_x.at[:, :, tile(d)], lambda d: gi_out.at[y])
    arrive(g_2)
    gx2[x] = (gy[0] + gy[1]) + (gy[2] + gy[3])
    g_3 = net.send("x", 1, gx2.at[x], gx2.at[x])
    g_3.wait_recv()
    gg_out[...] = gx2[0] + gx2[1]
    arrive(f_4)
    for copy in stores:
        copy.wait()
    net.finish()


def run_layer(tokens, cotangent, gain_row, visible, feats, w_q, w_o, w_kv):
    any_spec = pl.BlockSpec(memory_space=pl.ANY)
    vmem = pl.BlockSpec(memory_space=pltpu.VMEM)
    smem = pl.BlockSpec(memory_space=pltpu.SMEM)
    shape = jax.ShapeDtypeStruct
    b, f = (lambda *dims: pltpu.VMEM(dims, BF16)), (lambda *dims: pltpu.VMEM(dims, F32))
    return pl.pallas_call(
        layer_kernel,
        out_shape=(
            shape((4, 4, 16, D), BF16),
            shape((4, 4, 16, D), BF16),
            shape((TOK, 256), BF16),
            shape((TOK, 256), BF16),
            shape((256, 2048), BF16),
            shape((8, D), BF16),
            shape((8, 1024), F32),
            shape((4, 2, 4, 8, 256), F32),
        ),
        in_specs=[vmem, vmem, vmem, smem, vmem, any_spec, any_spec, any_spec],
        out_specs=(any_spec, any_spec, vmem, vmem, vmem, vmem, vmem, vmem),
        scratch_shapes=[
            b(4, 4, 16, D), b(4, 4, 16, D), b(D, 256), b(256, D), b(256, 2048),
            b(16, HALF), b(16, HALF), b(16, HALF), b(16, HALF),
            f(4, 2, 4, 128, HD), b(4, 2, 4, 128, HD),
            f(3, 4, 2, 128, HD), b(3, 2, 4, 128, HD),
            f(4, 2, 128, HD), b(2, 4, 128, HD),
            f(3, 2, 128, HD), b(3, 2, 128, HD),
            f(2, 128, HD), b(2, 128, HD),
            f(128, HD), b(128, HD),
            b(4, 128, HD), b(4, 128, HD),
            b(4, 128, HD), b(4, 128, HD), b(3, 128, HD), b(3, 128, HD),
            b(4, 2, 4, 128, HD), b(4, 2, 4, 128, HD),
            b(4, 4, 16, D),
            b(3, 4, 16, HALF), b(3, 4, 16, HALF),
            b(4, 16, HALF), b(4, 16, HALF),
            b(3, 16, HALF), b(3, 16, HALF),
            f(16, HALF), b(16, HALF), b(16, HALF),
            f(4, 128, 256), f(3, 128, 256),
            f(4, 32, 256), f(4, 32, 256), f(2, 4, 16, 256),
            f(4, 8, 1024), f(4, 8, 1024), f(2, 8, 1024),
            pltpu.SemaphoreType.DMA((NSEM,)),
            pltpu.SemaphoreType.DMA((NSEM,)),
            pltpu.SemaphoreType.DMA((5,)),
        ],
        compiler_params=pltpu.CompilerParams(
            collective_id=0, has_side_effects=True, vmem_limit_bytes=58 * 1024 * 1024
        ),
        cost_estimate=pl.CostEstimate(
            flops=6 * 10**9, bytes_accessed=20 * 2**20, transcendentals=2 * 256 * 512
        ),
        name="layer",
    )(tokens, cotangent, gain_row, visible, feats, w_q, w_o, w_kv)


def per_device(tokens, upstream, norm_gain, w_query, w_output, w_keyvalue, image_feats, visible):
    wide_rows = lax.all_gather(image_feats, "section", axis=0, tiled=True)
    mixed = lax.all_to_all(wide_rows, "mp", split_axis=1, concat_axis=0, tiled=True)
    feats = mixed.reshape(32, 4, 4, VCOLS).transpose(1, 0, 2, 3).reshape(512, VCOLS)
    feats = jnp.pad(feats, ((0, 0), (0, 256 - VCOLS)))
    normed, cotangent, attn, d_query, grad_kv, grad_x, grad_g, image = run_layer(
        tokens[0], upstream[0], norm_gain, visible, feats, w_query[0], w_output[0], w_keyvalue[0]
    )
    grad_q = lax.dot_general(normed.reshape(TOK, D), d_query, TN, preferred_element_type=F32)
    grad_out = lax.dot_general(attn, cotangent.reshape(TOK, D), TN, preferred_element_type=F32)
    odd = lax.axis_index("mp") % 2
    rows = lax.dynamic_slice_in_dim(image, odd * 4, 4, 3)[..., :VCOLS]
    grad_image = rows.transpose(3, 2, 1, 0, 4).reshape(4, 32 * VCOLS)
    return (
        grad_x[None],
        grad_g.reshape(1, D),
        grad_q.astype(BF16)[None],
        grad_out.astype(BF16)[None],
        grad_kv[None, :VCOLS],
        grad_image,
    )


def solution(mesh):
    placed = (
        P("section", "mp", None),
        P("section", "mp", None),
        P("section", None),
        P("section", None, "mp"),
        P("section", "mp", None),
        P("section", "mp", None),
        P(("section", "mp"), None),
        P(),
    )
    return jax.shard_map(
        per_device,
        mesh=mesh,
        in_specs=placed,
        out_specs=(
            P("section", "mp", None),
            P("section", None),
            P("section", None, "mp"),
            P("section", "mp", None),
            P("section", "mp", None),
            P(("section", "mp"), None),
        ),
        check_vma=False,
    )
```

time: 995 us -> 212 us (0.21)
  waiting for transfers between devices: 696 us -> 11.1 us
  blocking collectives: 212 us -> 5.95 us
  Pallas kernels: 0 us -> 165 us
  matrix products: 43.3 us -> 8.96 us
  between operations: 14.4 us -> 0.71 us
  other arithmetic: 13.4 us -> 0 us
    reduce_scatter x3 -> x0, waiting for transfers between devices: 382 us -> none  [the longest x1 186 us: per_device(): lax.psum_scatter(jnp.dot(rows, w_kv, preferred_element_type=jnp.float32),...]
    all_gather x4 -> x0, waiting for transfers between devices: 313 us -> none  [the longest x1 90.7 us: per_device(): stacked = lax.all_gather(pair_terms, 'mp', axis=1, tiled=True)]
    psum x1 -> x0, blocking collectives: 184 us -> none  [per_device(): grad_g = lax.psum(gain_part, 'mp')]
    pallas_call x0 -> x1, Pallas kernels: none -> 165 us  [run_layer(): pl.pallas_call(layer_kernel, out_shape=(shape((4, 4, 16, D), BF16), shape...]
    dot_general x13 -> x2, matrix products: 41 us -> 8.96 us  [the longest x1 5.66 us: per_device(): lax.dot_general(normed.reshape(TOK, D), d_query, TN, preferred_element_ty...]
    all_to_all x1 -> x0, blocking collectives: 21.8 us -> none  [per_device(): lax.all_to_all(wide_rows, 'mp', split_axis=1, concat_axis=0, tiled=True)]
    all_to_all x1, waiting for transfers between devices: 0.01 us -> 11.1 us  [per_device(): lax.all_to_all(wide_rows, 'mp', split_axis=1, concat_axis=0, tiled=True)]
  transfers between devices with their start and end apart: 8 -> 1, of which waited for: 7 -> 1; matrix products, arithmetic and copies ran while one was open for 5% -> 0% of each run, Pallas kernels for 0% -> 0%
where the time goes in v1:
time: 212 us; the launch traced here: 211 us
  Pallas kernels  165 us (78%)
  waiting for transfers between devices  11.1 us (5%)
  starting transfers between devices  10.9 us (5%)
  matrix products  8.96 us (4%)
  local copies, waits for them, and re-layouts  8.89 us (4%)
  blocking collectives  5.95 us (3%)
    pallas_call x1, Pallas kernels, run_layer(): pl.pallas_call(layer_kernel, out_shape=(shape((4, 4, 16, D), BF16), shape...  165 us
    all_to_all x1, waiting for transfers between devices, per_device(): lax.all_to_all(wide_rows, 'mp', split_axis=1, concat_axis=0, tiled=True)  11.1 us
    all_to_all x1, starting transfers between devices, per_device(): lax.all_to_all(wide_rows, 'mp', split_axis=1, concat_axis=0, tiled=True)  10.9 us
    all_gather x1, blocking collectives, per_device(): wide_rows = lax.all_gather(image_feats, 'section', axis=0, tiled=True)  5.95 us
    dot_general x1, matrix products, per_device(): lax.dot_general(normed.reshape(TOK, D), d_query, TN, preferred_element_ty...  5.66 us
  transfers between devices with their start and end apart: 1, of which 1 were waited for; matrix products, arithmetic and copies ran while one was open for 0% of the time, Pallas kernels for 0%

profile of v1, /device:TPU:0, one launch (start us, length us, event | category | flops | bytes accessed | tf_op | source)
XLA Modules:
  0.0 211.3 jit_solution(6430678453627612901)
XLA Ops:
  0.6 6.0 %all-gather = bf16[4,4,7680]{2,1,0:T(4,128)(2,1)S(1)} all-gather(bf16[1,4,7680]{2,1,0:T(4,128)(2,1)} %bitcast.33), channel_id=1, replica_groups=mesh['section'=4,'mp'=32] {'section'}, dimensions={0}, use_global_device_ids=true | all-gather | bytes 307200 | tf_op jit(solution)/shard_map/all_gather | solution.py:463
  6.6 0.6 all_to_all.12
  7.2 0.9 copy.16
  8.1 10.9 %all-to-all-start = ((bf16[16,32,240]{2,0,1:T(8,128)(2,1)}), bf16[16,32,240]{2,0,1:T(8,128)(2,1)S(1)}, u32[]{:S(2)}, u32[]{:S(2)}) async-start(bf16[16,32,240]{2,0,1:T(8,128)(2,1)} %copy.16), calls=%async_computation | async-start | bytes 524288 | tf_op jit(solution)/shard_map/all_to_all | solution.py:464
  19.0 11.1 %all-to-all-done = bf16[16,32,240]{2,0,1:T(8,128)(2,1)S(1)} async-done(((bf16[16,32,240]{2,0,1:T(8,128)(2,1)}), bf16[16,32,240]{2,0,1:T(8,128)(2,1)S(1)}, u32[]{:S(2)}, u32[]{:S(2)}) %all-to-all-start) | async-done | bytes 245792 | tf_op jit(solution)/shard_map/all_to_all | solution.py:464
  30.1 0.1 copy.17
  30.2 0.2 copy.18
  30.4 0.2 reshape.35
  30.5 0.7 pad.4.feat_ref
  31.3 164.7 %layer.1 = (bf16[4,4,16,8192]{3,2,1,0:T(8,128)(2,1)}, bf16[4,4,16,8192]{3,2,1,0:T(8,128)(2,1)}, bf16[256,256]{1,0:T(8,128)(2,1)}, bf16[256,256]{1,0:T(8,128)(2,1...) custom-call(bf16[8,8192]{1,0:T(8,128)(2,1)} %bitcast.39, ...), custom_call_target="tpu_custom_call" | custom-call | flops 6000000000 | bytes 20971520 | tf_op jit(solution)/shard_map/layer/pallas_call | solution.py:414
  196.0 1.4 copy.20
  197.4 1.0 dynamic-slice_bitcast_fusion
  198.4 0.1 copy.19
  198.5 0.9 reshape.39
  199.4 2.2 %slice_bitcast_fusion = bf16[1,240,2048]{2,1,0:T(8,128)(2,1)} fusion(bf16[256,2048]{1,0:T(8,128)(2,1)} %get-tuple-element.20), kind=kLoop, calls=%fused_computation.4 | loop fusion | bytes 1966080 | tf_op jit(solution)/shard_map/broadcast_in_dim | solution.py:480
  201.6 0.0 copy-start
  201.6 0.0 copy-start.1
  201.6 5.7 %fusion = bf16[1,8192,256]{2,1,0:T(8,128)(2,1)} fusion(bf16[256,8192]{1,0:T(8,128)(2,1)} %bitcast.29, bf16[256,256]{1,0:T(8,128)(2,1)} %get-tuple-element.17), kind=kOutput, calls=%fused_computation.2 | convolution fusion | flops 1075838976 | bytes 8519680 | tf_op jit(solution)/shard_map/dot_general | solution.py:470
  207.3 0.0 copy-done
  207.3 0.0 copy-done.1
  207.3 0.0 copy-start.2
  207.3 3.3 %fusion.1 = bf16[1,256,8192]{2,1,0:T(8,128)(2,1)} fusion(bf16[256,256]{1,0:T(8,128)(2,1)S(1)} %copy-done.1, bf16[256,8192]{1,0:T(8,128)(2,1)S(1)} %bitcast.30), kind=kOutput, calls=%fused_computation.3 | convolution fusion | flops 1075838976 | bytes 8519680 | tf_op jit(solution)/shard_map/dot_general | solution.py:471
  210.6 0.0 copy-done.2
  210.6 0.7 copy.22
Async XLA Ops:
  8.1 22.0 %all-to-all-start = ((bf16[16,32,240]{2,0,1:T(8,128)(2,1)}), bf16[16,32,240]{2,0,1:T(8,128)(2,1)S(1)}, u32[]{:S(2)}, u32[]{:S(2)}) async-start(bf16[16,32,240]{2,0,1:T(8,128)(2,1)} %copy.16), calls=%async_computation | async-start | bytes 524288 | tf_op jit(solution)/shard_map/all_to_all | solution.py:464
  201.6 5.7 %copy-start = (bf16[4,4,16,8192]{3,2,1,0:T(8,128)(2,1)S(1)}, bf16[4,4,16,8192]{3,2,1,0:T(8,128)(2,1)}, u32[]{:S(2)}) copy-start(bf16[4,4,16,8192]{3,2,1,0:T(8,128)(2,1)} %get-tuple-element.19) | copy-start | bytes 12582916
  201.6 5.7 %copy-start.1 = (bf16[256,256]{1,0:T(8,128)(2,1)S(1)}, bf16[256,256]{1,0:T(8,128)(2,1)}, u32[]{:S(2)}) copy-start(bf16[256,256]{1,0:T(8,128)(2,1)} %get-tuple-element.18) | copy-start | bytes 393220
  207.3 3.3 %copy-start.2 = (bf16[8,8192]{1,0:T(8,128)(2,1)S(1)}, bf16[8,8192]{1,0:T(8,128)(2,1)}, u32[]{:S(2)}) copy-start(bf16[8,8192]{1,0:T(8,128)(2,1)} %get-tuple-element.14) | copy-start | bytes 393220

commit v2 on v1

--- a/solution.py
+++ b/solution.py
@@ -15,7 +15,7 @@
 HD = 128
 VCOLS = 240
 SCALE = HD ** (-0.5)
-NSEM = 96
+NSEM = 128
 
 NT = (((1,), (1,)), ((), ()))
 TN = (((0,), (0,)), ((), ()))
@@ -84,14 +84,15 @@
 
 
 def layer_kernel(
-    tok_ref, cot_ref, gain_ref, vis_ref, feat_ref, wq_hbm, wo_hbm, wkv_hbm,
+    tok_ref, cot_ref, gain_ref, vis_ref, unit_ref, wq_hbm, wo_hbm, wkv_hbm,
     n_out, c_out, attn_out, dq_out, gkv_out, gx_out, gg_out, gi_out,
     n_all, c_all, wq, wo, wkv,
+    u_y, u_z, u_x, feat_all,
     fold_n, fold_c, from_n, from_c,
     pk, pv, k1, v1, ks1, vs1, k2, v2, ks2, vs2, kx, vx, keys, values,
     dk, dv, rk, rv, dkg, dvg,
     pd, da1, db1, sa1, sb1, da2, db2, own_d, fold_d, from_d,
-    df, dfr, img_s, img_z, img_x, gz, gy, gx2,
+    df, dfr, img_s, img_z, img_x, gi_all, gain_part, gz, gy, gx2,
     send_sems, recv_sems, local_sems,
 ):
     net = Links(send_sems, recv_sems)
@@ -104,6 +105,9 @@
         loads.append(copy)
     net.barrier()
 
+    u_y[y] = unit_ref[:, :, y]
+    u_1 = net.ring("y", lambda d: unit_ref.at[:, :, net.coord("y", d)], lambda d: u_y.at[y])
+
     xf = tok_ref[...].astype(F32)
     rinv = lax.rsqrt(jnp.mean(xf * xf, axis=-1, keepdims=True) + 1e-05)
 
@@ -120,20 +124,10 @@
 
     pl.loop(0, HALF // CHUNK)(fold_step)
     x_n = net.send("x", 1, fold_n, from_n)
+    arrive(u_1)
+    u_z[z] = u_y[:, z]
+    u_2 = net.ring("z", lambda d: u_y.at[:, net.coord("z", d)], lambda d: u_z.at[z])
     x_c = net.send("x", 1, fold_c, from_c)
-
-    loads[0].wait()
-
-    def kv_step(h):
-        cols = pl.ds(pl.multiple_of(h * HD, HD), HD)
-        vcols = pl.ds(pl.multiple_of(1024 + h * HD, HD), HD)
-        feats = feat_ref[...]
-        pk[h // 2, h % 2] = dot(feats, wkv[:, cols]).reshape(4, 128, HD)
-        pv[h // 2, h % 2] = dot(feats, wkv[:, vcols]).astype(BF16).reshape(4, 128, HD)
-
-    pl.loop(0, 8)(kv_step)
-    k_1 = net.ring("y", lambda d: pk.at[:, :, net.coord("y", d)], lambda d: k1.at[d - 1])
-    v_1 = net.ring("z", lambda d: pv.at[net.coord("z", d)], lambda d: v1.at[d - 1])
 
     def unfold(folded, received, full):
         def step(i):
@@ -165,16 +159,44 @@
         part_b = full.at[z, :, :, b_cols]
         return out + net.ring("z", lambda d: part_b, lambda d: part_b)
 
+
+    arrive(u_2)
+    u_x[x] = u_z[:, :, x]
+    u_3 = net.send("x", 1, u_z.at[:, :, 1 - x], u_x.at[x])
     x_n.wait_recv()
     unfold(fold_n, from_n, n_all)
     n_1 = gather_start(n_all)
 
+    u_3.wait_recv()
+    units = u_x[...].reshape(256, HD).astype(BF16)
+    row = lax.broadcasted_iota(jnp.int32, (128, 256), 0)
+    col = lax.broadcasted_iota(jnp.int32, (128, 256), 1)
+    at = (((row // 16) % 2 * 4 + row // 32) * 4 + (row // 4) % 4) * 8 + row % 4
+    for half in range(2):
+        pick = jnp.where(col == at + 4 * half, 1.0, 0.0).astype(BF16)
+        feat_all[s, :, half * HD : (half + 1) * HD] = dot(pick, units).astype(BF16)
+    f_0 = net.ring("s", lambda d: feat_all.at[s], lambda d: feat_all.at[s])
+    arrive(f_0)
+
+    loads[0].wait()
+
+    def kv_step(h):
+        cols = pl.ds(pl.multiple_of(h * HD, HD), HD)
+        vcols = pl.ds(pl.multiple_of(1024 + h * HD, HD), HD)
+        feats = feat_all[...].reshape(512, 256)
+        pk[h // 2, h % 2] = dot(feats, wkv[:, cols]).astype(BF16).reshape(4, 128, HD)
+        pv[h // 2, h % 2] = dot(feats, wkv[:, vcols]).astype(BF16).reshape(4, 128, HD)
+
+    pl.loop(0, 8)(kv_step)
+    k_1 = net.ring("y", lambda d: pk.at[:, :, net.coord("y", d)], lambda d: k1.at[d - 1])
+    v_1 = net.ring("z", lambda d: pv.at[net.coord("z", d)], lambda d: v1.at[d - 1])
+
     arrive(k_1)
     for a in range(4):
         for b in range(2):
-            total = pk[a, b, y]
+            total = pk[a, b, y].astype(F32)
             for d in range(3):
-                total += k1[d, a, b]
+                total += k1[d, a, b].astype(F32)
             ks1[a, b] = total
     k_2 = net.ring("z", lambda d: ks1.at[net.coord("z", d)], lambda d: k2.at[d - 1])
     arrive(v_1)
@@ -183,7 +205,7 @@
             total = pv[z, b, c].astype(F32)
             for d in range(3):
                 total += v1[d, b, c].astype(F32)
-            vs1[b, c] = total.astype(BF16)
+            vs1[b, c] = total
     v_2 = net.ring("y", lambda d: vs1.at[:, net.coord("y", d)], lambda d: v2.at[d - 1])
 
     n_2 = gather_on(n_all, *n_1)
@@ -194,19 +216,19 @@
     arrive(v_2)
     for b in range(2):
         total = ks1[z, b]
-        vtotal = vs1[b, y].astype(F32)
+        vtotal = vs1[b, y]
         for d in range(3):
             total += k2[d, b]
-            vtotal += v2[d, b].astype(F32)
+            vtotal += v2[d, b]
         ks2[b] = total
-        vs2[b] = vtotal.astype(BF16)
+        vs2[b] = vtotal
     k_x = net.send("x", 1, ks2.at[1 - x], kx)
     v_x = net.send("x", 1, vs2.at[1 - x], vx)
     c_1 = gather_start(c_all)
     k_x.wait_recv()
     v_x.wait_recv()
     keys[y] = (ks2[x] + kx[...]).astype(BF16)
-    values[y] = (vs2[x].astype(F32) + vx[...].astype(F32)).astype(BF16)
+    values[y] = (vs2[x] + vx[...]).astype(BF16)
     k_3 = net.ring("y", lambda d: keys.at[y], lambda d: keys.at[y])
     v_3 = net.ring("y", lambda d: values.at[y], lambda d: values.at[y])
 
@@ -272,6 +294,8 @@
     def d_normed_step(cols):
         part = dot(dq_out[...], wq[cols, :], NT)
         pd[:, :, :, cols] = part.astype(BF16).reshape(4, 4, 16, CHUNK)
+        normed = n_all[:, :, :, cols].reshape(TOK, CHUNK).astype(F32)
+        gain_part[:, cols] = jnp.sum(part * normed, axis=0, keepdims=True) / gain_ref[:, cols]
 
     columns(0, HALF, d_normed_step)
     da_1 = net.ring(
@@ -279,6 +303,9 @@
     )
     columns(HALF, D, d_normed_step)
     db_1 = net.ring("z", lambda d: pd.at[net.coord("z", d), :, :, b_cols], lambda d: db1.at[d - 1])
+    for i in range(8):
+        gz[z, i : i + 1, :] = gain_part[:, i * 1024 : (i + 1) * 1024]
+    g_1 = net.ring("z", lambda d: gz.at[z], lambda d: gz.at[z])
 
     arrive(dk_1)
     arrive(dv_1)
@@ -297,6 +324,9 @@
     pair_k, pair_v = dkg.at[z, :, y], dvg.at[z, :, y]
     dk_3 = net.ring("z", lambda d: pair_k, lambda d: pair_k)
     dv_3 = net.ring("y", lambda d: pair_v, lambda d: pair_v)
+    arrive(g_1)
+    gy[y] = (gz[0] + gz[1]) + (gz[2] + gz[3])
+    g_2 = net.ring("y", lambda d: gy.at[y], lambda d: gy.at[y])
     arrive(dk_3)
     line_k = dkg.at[:, :, y]
     dk_4 = net.ring("y", lambda d: line_k, lambda d: line_k)
@@ -304,6 +334,9 @@
     line_v = dvg.at[z]
     dv_4 = net.ring("z", lambda d: line_v, lambda d: line_v)
 
+    arrive(g_2)
+    gx2[x] = (gy[0] + gy[1]) + (gy[2] + gy[3])
+    g_3 = net.send("x", 1, gx2.at[x], gx2.at[x])
     arrive(da_1)
 
     def sum_a(i):
@@ -330,7 +363,7 @@
 
     arrive(dk_4)
     arrive(dv_4)
-    feats = feat_ref[...]
+    feats = feat_all[...].reshape(512, 256)
     d_feats = jnp.zeros((512, 256), F32)
     for h in range(8):
         for at, full in ((h * HD, dkg), (1024 + h * HD, dvg)):
@@ -367,6 +400,8 @@
     img_z[z] = img_s[z]
     f_2 = net.ring("z", lambda d: img_s.at[net.coord("z", d)], lambda d: img_z.at[z])
 
+    g_3.wait_recv()
+    gg_out[...] = gx2[0] + gx2[1]
     d_x.wait_recv()
     both = own_d[...] + from_d[...].astype(F32)
     dn = jnp.concatenate([both[:8], both[8:]], axis=1)
@@ -375,37 +410,27 @@
     gx_out[...] = (
         rinv * scaled - xf * rinv * rinv * rinv * jnp.mean(xf * scaled, axis=-1, keepdims=True)
     ).astype(BF16)
-    gain = jnp.sum(dn * xf * rinv, axis=0, keepdims=True)
-    for i in range(8):
-        gz[z, i : i + 1, :] = gain[:, i * 1024 : (i + 1) * 1024]
-    g_1 = net.ring("z", lambda d: gz.at[z], lambda d: gz.at[z])
-
     arrive(f_2)
     img_x[x] = img_z[:, pl.ds(pl.multiple_of(x * 16, 16), 16), :]
     far = pl.ds(pl.multiple_of((1 - x) * 16, 16), 16)
     f_3 = net.send("x", 1, img_z.at[:, far], img_x.at[x])
-    arrive(g_1)
-    gy[y] = (gz[0] + gz[1]) + (gz[2] + gz[3])
-    g_2 = net.ring("y", lambda d: gy.at[y], lambda d: gy.at[y])
     f_3.wait_recv()
 
     def tile(d):
         return pl.ds(pl.multiple_of((net.coord("y", d) // 2) * 8, 8), 8)
 
-    gi_out[y] = img_x[:, :, tile(0), :]
-    f_4 = net.ring("y", lambda d: img_x.at[:, :, tile(d)], lambda d: gi_out.at[y])
-    arrive(g_2)
-    gx2[x] = (gy[0] + gy[1]) + (gy[2] + gy[3])
-    g_3 = net.send("x", 1, gx2.at[x], gx2.at[x])
-    g_3.wait_recv()
-    gg_out[...] = gx2[0] + gx2[1]
+    gi_all[y] = img_x[:, :, tile(0), :]
+    f_4 = net.ring("y", lambda d: img_x.at[:, :, tile(d)], lambda d: gi_all.at[y])
     arrive(f_4)
+    for m in range(32):
+        tile_m = gi_all[m % 4, (m // 4) % 2, m // 8]
+        gi_out[:, m * VCOLS : (m + 1) * VCOLS] = jnp.where(y % 2 == 0, tile_m[:4], tile_m[4:])[:, :VCOLS]
     for copy in stores:
         copy.wait()
     net.finish()
 
 
-def run_layer(tokens, cotangent, gain_row, visible, feats, w_q, w_o, w_kv):
+def run_layer(tokens, cotangent, gain_row, visible, units, w_q, w_o, w_kv):
     any_spec = pl.BlockSpec(memory_space=pl.ANY)
     vmem = pl.BlockSpec(memory_space=pltpu.VMEM)
     smem = pl.BlockSpec(memory_space=pltpu.SMEM)
@@ -421,19 +446,20 @@
             shape((256, 2048), BF16),
             shape((8, D), BF16),
             shape((8, 1024), F32),
-            shape((4, 2, 4, 8, 256), F32),
+            shape((4, 32 * VCOLS), F32),
         ),
         in_specs=[vmem, vmem, vmem, smem, vmem, any_spec, any_spec, any_spec],
         out_specs=(any_spec, any_spec, vmem, vmem, vmem, vmem, vmem, vmem),
         scratch_shapes=[
             b(4, 4, 16, D), b(4, 4, 16, D), b(D, 256), b(256, D), b(256, 2048),
+            f(4, 4, 2, 8, HD), f(4, 4, 2, 8, HD), f(2, 4, 4, 8, HD), b(4, 128, 256),
             b(16, HALF), b(16, HALF), b(16, HALF), b(16, HALF),
-            f(4, 2, 4, 128, HD), b(4, 2, 4, 128, HD),
-            f(3, 4, 2, 128, HD), b(3, 2, 4, 128, HD),
-            f(4, 2, 128, HD), b(2, 4, 128, HD),
-            f(3, 2, 128, HD), b(3, 2, 128, HD),
-            f(2, 128, HD), b(2, 128, HD),
-            f(128, HD), b(128, HD),
+            b(4, 2, 4, 128, HD), b(4, 2, 4, 128, HD),
+            b(3, 4, 2, 128, HD), b(3, 2, 4, 128, HD),
+            f(4, 2, 128, HD), f(2, 4, 128, HD),
+            f(3, 2, 128, HD), f(3, 2, 128, HD),
+            f(2, 128, HD), f(2, 128, HD),
+            f(128, HD), f(128, HD),
             b(4, 128, HD), b(4, 128, HD),
             b(4, 128, HD), b(4, 128, HD), b(3, 128, HD), b(3, 128, HD),
             b(4, 2, 4, 128, HD), b(4, 2, 4, 128, HD),
@@ -443,8 +469,8 @@
             b(3, 16, HALF), b(3, 16, HALF),
             f(16, HALF), b(16, HALF), b(16, HALF),
             f(4, 128, 256), f(3, 128, 256),
-            f(4, 32, 256), f(4, 32, 256), f(2, 4, 16, 256),
-            f(4, 8, 1024), f(4, 8, 1024), f(2, 8, 1024),
+            f(4, 32, 256), f(4, 32, 256), f(2, 4, 16, 256), f(4, 2, 4, 8, 256),
+            f(1, D), f(4, 8, 1024), f(4, 8, 1024), f(2, 8, 1024),
             pltpu.SemaphoreType.DMA((NSEM,)),
             pltpu.SemaphoreType.DMA((NSEM,)),
             pltpu.SemaphoreType.DMA((5,)),
@@ -456,28 +482,55 @@
             flops=6 * 10**9, bytes_accessed=20 * 2**20, transcendentals=2 * 256 * 512
         ),
         name="layer",
-    )(tokens, cotangent, gain_row, visible, feats, w_q, w_o, w_kv)
+    )(tokens, cotangent, gain_row, visible, units, w_q, w_o, w_kv)
+
+
+def weight_kernel(n_ref, c_ref, attn_ref, dq_ref, gkv_ref, gq_ref, go_ref, gk_ref):
+    width = n_ref.shape[-1]
+    gq_ref[...] = dot(n_ref[...].reshape(TOK, width), dq_ref[...], TN).astype(BF16)
+    go_ref[...] = dot(attn_ref[...], c_ref[...].reshape(TOK, width), TN).astype(BF16)
+    gk_ref[...] = gkv_ref[:VCOLS, :]
+
+
+def weight_grads(normed, cotangent, attn, d_query, grad_kv):
+    steps = 8
+    width, kv_width = D // steps, 2048 // steps
+    shape = jax.ShapeDtypeStruct
+    wide = pl.BlockSpec((4, 4, 16, width), lambda i: (0, 0, 0, i))
+    whole = pl.BlockSpec((TOK, 256), lambda i: (0, 0))
+    return pl.pallas_call(
+        weight_kernel,
+        grid=(steps,),
+        out_shape=(
+            shape((D, 256), BF16),
+            shape((256, D), BF16),
+            shape((VCOLS, 2048), BF16),
+        ),
+        in_specs=[wide, wide, whole, whole, pl.BlockSpec((256, kv_width), lambda i: (0, i))],
+        out_specs=(
+            pl.BlockSpec((width, 256), lambda i: (i, 0)),
+            pl.BlockSpec((256, width), lambda i: (0, i)),
+            pl.BlockSpec((VCOLS, kv_width), lambda i: (0, i)),
+        ),
+        compiler_params=pltpu.CompilerParams(vmem_limit_bytes=32 * 1024 * 1024),
+        name="weight_grads",
+    )(normed, cotangent, attn, d_query, grad_kv)
 
 
 def per_device(tokens, upstream, norm_gain, w_query, w_output, w_keyvalue, image_feats, visible):
-    wide_rows = lax.all_gather(image_feats, "section", axis=0, tiled=True)
-    mixed = lax.all_to_all(wide_rows, "mp", split_axis=1, concat_axis=0, tiled=True)
-    feats = mixed.reshape(32, 4, 4, VCOLS).transpose(1, 0, 2, 3).reshape(512, VCOLS)
-    feats = jnp.pad(feats, ((0, 0), (0, 256 - VCOLS)))
-    normed, cotangent, attn, d_query, grad_kv, grad_x, grad_g, image = run_layer(
-        tokens[0], upstream[0], norm_gain, visible, feats, w_query[0], w_output[0], w_keyvalue[0]
+    units = image_feats.astype(F32).reshape(4, 32, VCOLS)
+    units = jnp.pad(units, ((0, 0), (0, 0), (0, 256 - VCOLS))).reshape(4, 32, 2, HD)
+    units = units.transpose(1, 2, 0, 3).reshape(4, 2, 4, 8, HD)
+    normed, cotangent, attn, d_query, grad_kv, grad_x, grad_g, grad_image = run_layer(
+        tokens[0], upstream[0], norm_gain, visible, units, w_query[0], w_output[0], w_keyvalue[0]
     )
-    grad_q = lax.dot_general(normed.reshape(TOK, D), d_query, TN, preferred_element_type=F32)
-    grad_out = lax.dot_general(attn, cotangent.reshape(TOK, D), TN, preferred_element_type=F32)
-    odd = lax.axis_index("mp") % 2
-    rows = lax.dynamic_slice_in_dim(image, odd * 4, 4, 3)[..., :VCOLS]
-    grad_image = rows.transpose(3, 2, 1, 0, 4).reshape(4, 32 * VCOLS)
+    grad_q, grad_out, grad_kv = weight_grads(normed, cotangent, attn, d_query, grad_kv)
     return (
         grad_x[None],
         grad_g.reshape(1, D),
-        grad_q.astype(BF16)[None],
-        grad_out.astype(BF16)[None],
-        grad_kv[None, :VCOLS],
+        grad_q[None],
+        grad_out[None],
+        grad_kv[None],
         grad_image,
     )
 

time: 212 us -> 193 us (0.910)
  Pallas kernels: 165 us -> 180 us
  waiting for transfers between devices: 11.1 us -> 0 us
  starting transfers between devices: 10.9 us -> 0 us
  matrix products: 8.96 us -> 0 us
  blocking collectives: 5.95 us -> 0 us
  local copies, waits for them, and re-layouts: 8.89 us -> 11.9 us
    all_to_all x1 -> x0, waiting for transfers between devices: 11.1 us -> none  [per_device(): lax.all_to_all(wide_rows, 'mp', split_axis=1, concat_axis=0, tiled=True)]
    all_to_all x1 -> x0, starting transfers between devices: 10.9 us -> none  [per_device(): lax.all_to_all(wide_rows, 'mp', split_axis=1, concat_axis=0, tiled=True)]
    dot_general x2 -> x0, matrix products: 8.96 us -> none  [the longest x1 5.66 us: per_device(): lax.dot_general(normed.reshape(TOK, D), d_query, TN, preferred_element_ty...]
    pallas_call x1, Pallas kernels: 165 us -> 173 us  [run_layer(): pl.pallas_call(layer_kernel, out_shape=(shape((4, 4, 16, D), BF16), shape...]
    unnamed x8 -> x17, local copies, waits for them, and re-layouts: 2.07 us -> 10.1 us
    pallas_call x0 -> x1, Pallas kernels: none -> 6.92 us  [weight_grads(): pl.pallas_call(weight_kernel, grid=(steps,), out_shape=(shape((D, 256), B...]
    all_gather x1 -> x0, blocking collectives: 5.95 us -> none  [per_device(): wide_rows = lax.all_gather(image_feats, 'section', axis=0, tiled=True)]
    broadcast_in_dim x1 -> x0, local copies, waits for them, and re-layouts: 2.25 us -> none  [per_device(): grad_kv[None, :VCOLS]]
  transfers between devices with their start and end apart: 1 -> 0, of which waited for: 1 -> 0; matrix products, arithmetic and copies ran while one was open for 0% -> 0% of each run, Pallas kernels for 0% -> 0%
where the time goes in v2:
time: 193 us
  Pallas kernels  180 us (93%)
  local copies, waits for them, and re-layouts  11.9 us (6%)
    pallas_call x1, Pallas kernels, run_layer(): pl.pallas_call(layer_kernel, out_shape=(shape((4, 4, 16, D), BF16), shape...  173 us
    unnamed x17, local copies, waits for them, and re-layouts  10.1 us
    pallas_call x1, Pallas kernels, weight_grads(): pl.pallas_call(weight_kernel, grid=(steps,), out_shape=(shape((D, 256), B...  6.92 us

profile of v2, /device:TPU:0, one launch (start us, length us, event | category | flops | bytes accessed | tf_op | source)
XLA Modules:
  0.0 192.8 jit_solution(1154735650061076423)
XLA Ops:
  0.6 1.0 reshape.28
  1.6 0.1 reshape.37
  1.7 0.7 copy.14
  2.5 173.3 %layer.1 = (bf16[4,4,16,8192]{3,2,1,0:T(8,128)(2,1)}, bf16[4,4,16,8192]{3,2,1,0:T(8,128)(2,1)}, bf16[256,256]{1,0:T(8,128)(2,1)}, bf16[256,256]{1,0:T(8,128)(2,1...) custom-call(bf16[8,8192]{1,0:T(8,128)(2,1)} %bitcast.25, ...), custom_call_target="tpu_custom_call" | custom-call | flops 6000000000 | bytes 20971520 | tf_op jit(solution)/shard_map/layer/pallas_call | solution.py:439
  175.8 1.4 copy.15
  177.2 0.0 copy-start
  177.2 2.2 %copy-done = bf16[4,4,16,8192]{3,2,1,0:T(8,128)(2,1)S(1)} copy-done((bf16[4,4,16,8192]{3,2,1,0:T(8,128)(2,1)S(1)}, bf16[4,4,16,8192]{3,2,1,0:T(8,128)(2,1)}, u32[]{:S(2)}) %copy-start) | copy-done | bytes 4194328
  179.4 0.0 copy-start.1
  179.4 2.2 %copy-done.1 = bf16[4,4,16,8192]{3,2,1,0:T(8,128)(2,1)S(1)} copy-done((bf16[4,4,16,8192]{3,2,1,0:T(8,128)(2,1)S(1)}, bf16[4,4,16,8192]{3,2,1,0:T(8,128)(2,1)}, u32[]{:S(2)}) %copy-start.1) | copy-done | bytes 4194328
  181.6 0.0 copy-start.2
  181.6 1.2 copy-done.2
  182.8 0.0 copy-start.3
  182.8 0.9 copy-done.3
  183.7 0.0 copy-start.4
  183.7 0.9 copy-done.4
  184.6 0.0 copy-start.5
  184.6 0.0 copy-start.6
  184.6 6.9 %weight_grads.1 = (bf16[8192,256]{1,0:T(8,128)(2,1)}, bf16[256,8192]{1,0:T(8,128)(2,1)}, bf16[240,2048]{1,0:T(8,128)(2,1)}) custom-call(bf16[4,4,16,8192]{3,2,1,0:T(8,128)(2,1)S(1)} %copy-done, bf16[4,4,16,8192]{3,2,1,0:T(8,128)(2,1)S(1)} %copy-done.1, bf16[256,256]{1,0:T(8,128)(2,1)S(1)} %copy-done.3, bf16[256,256]{1,0:T(8,128)(2,1)S(1)} %copy-done.4, ...), custom_call_target="tpu_custom_call" | custom-call | tf_op jit(solution)/shard_map/weight_grads/pallas_call | solution.py:501
  191.5 0.0 copy-done.5
  191.5 0.7 copy.18
  192.2 0.0 copy-done.6
  192.2 0.6 copy.19
  (1 shorter events, 0.0 us)
Async XLA Ops:
  177.2 2.2 %copy-start = (bf16[4,4,16,8192]{3,2,1,0:T(8,128)(2,1)S(1)}, bf16[4,4,16,8192]{3,2,1,0:T(8,128)(2,1)}, u32[]{:S(2)}) copy-start(bf16[4,4,16,8192]{3,2,1,0:T(8,128)(2,1)} %get-tuple-element.19.n_ref) | copy-start | bytes 12582916
  179.4 2.2 %copy-start.1 = (bf16[4,4,16,8192]{3,2,1,0:T(8,128)(2,1)S(1)}, bf16[4,4,16,8192]{3,2,1,0:T(8,128)(2,1)}, u32[]{:S(2)}) copy-start(bf16[4,4,16,8192]{3,2,1,0:T(8,128)(2,1)} %get-tuple-element.20.c_ref) | copy-start | bytes 12582916
  181.6 1.2 copy-start.2
  182.8 0.9 copy-start.3
  183.7 0.9 copy-start.4
  184.6 6.9 %copy-start.5 = (bf16[8,8192]{1,0:T(8,128)(2,1)S(1)}, bf16[8,8192]{1,0:T(8,128)(2,1)}, u32[]{:S(2)}) copy-start(bf16[8,8192]{1,0:T(8,128)(2,1)} %get-tuple-element.17) | copy-start | bytes 393220
  184.6 7.6 %copy-start.6 = (f32[4,7680]{1,0:T(4,128)S(1)}, f32[4,7680]{1,0:T(4,128)}, u32[]{:S(2)}) copy-start(f32[4,7680]{1,0:T(4,128)} %get-tuple-element.39) | copy-start | bytes 368644

commit v3 on v2

--- a/solution.py
+++ b/solution.py
@@ -11,11 +11,12 @@
 TOK = 256
 D = 8192
 HALF = D // 2
+QUART = D // 4
 CHUNK = 1024
 HD = 128
 VCOLS = 240
 SCALE = HD ** (-0.5)
-NSEM = 128
+NSEM = 192
 
 NT = (((1,), (1,)), ((), ()))
 TN = (((0,), (0,)), ((), ()))
@@ -77,6 +78,46 @@
         copy.wait_recv()
 
 
+class Gather:
+    def __init__(self, net, full, first, second, start):
+        self.net, self.full, self.first, self.second = net, full, first, second
+        self.cols = pl.ds(start, HALF)
+        self.sub = (pl.ds(start, QUART), pl.ds(start + QUART, QUART))
+
+    def block(self, i, j, cols):
+        i, j = self.net.coord(self.first, i), self.net.coord(self.second, j)
+        return self.full.at[i, j, :, cols] if self.first == "z" else self.full.at[j, i, :, cols]
+
+    def push(self, axis, d, i, j, cols):
+        block = self.block(i, j, cols)
+        return self.net.send(axis, d, block, block)
+
+    def start(self):
+        self.near = [self.push(self.first, d, 0, 0, self.cols) for d in (1, 3)]
+        self.lines = [[self.push(self.second, d, 0, 0, self.cols) for d in (1, 3)]]
+
+    def middle(self):
+        self.far = []
+        for copy, d, sub in zip(self.near, (1, 3), self.sub):
+            copy.wait_recv()
+            self.far.append(self.push(self.first, d, 4 - d, 0, sub))
+            self.lines.append([self.push(self.second, e, 4 - d, 0, self.cols) for e in (1, 3)])
+
+    def spread(self):
+        arrive(self.far)
+        self.lines.append([self.push(self.second, e, 2, 0, self.cols) for e in (1, 3)])
+
+    def forward(self):
+        self.last = []
+        for i, line in zip((0, 3, 1, 2), self.lines):
+            for copy, d, sub in zip(line, (1, 3), self.sub):
+                copy.wait_recv()
+                self.last.append(self.push(self.second, d, i, 4 - d, sub))
+
+    def end(self):
+        arrive(self.last)
+
+
 def columns(start, stop, body, step=CHUNK):
     @pl.loop(0, (stop - start) // step)
     def _(i):
@@ -89,9 +130,9 @@
     n_all, c_all, wq, wo, wkv,
     u_y, u_z, u_x, feat_all,
     fold_n, fold_c, from_n, from_c,
-    pk, pv, k1, v1, ks1, vs1, k2, v2, ks2, vs2, kx, vx, keys, values,
+    feat_t, pk, pv, k_y, k_z, v_y, v_z, kv_1, kv_2, kv_3, kv_4, keys, values,
     dk, dv, rk, rv, dkg, dvg,
-    pd, da1, db1, sa1, sb1, da2, db2, own_d, fold_d, from_d,
+    pd, via_a, via_b, relay_a, relay_b, near_a, near_b, sa1, sb1, da2, db2, own_d, fold_d, from_d,
     df, dfr, img_s, img_z, img_x, gi_all, gain_part, gz, gy, gx2,
     send_sems, recv_sems, local_sems,
 ):
@@ -114,20 +155,21 @@
     def normed_at(cols):
         return tok_ref[:, cols].astype(F32) * rinv * gain_ref[:, cols]
 
-    def fold_step(i):
-        lo = pl.ds(pl.multiple_of(i * CHUNK, CHUNK), CHUNK)
-        hi = pl.ds(pl.multiple_of(HALF + i * CHUNK, CHUNK), CHUNK)
-        fold_n[:, lo] = jnp.concatenate([normed_at(lo), normed_at(hi)], axis=0).astype(BF16)
-        fold_c[:, lo] = jnp.concatenate(
-            [cot_ref[:, lo].astype(F32), cot_ref[:, hi].astype(F32)], axis=0
-        ).astype(BF16)
-
-    pl.loop(0, HALF // CHUNK)(fold_step)
+    def fold_step(at, into):
+        def step(i):
+            lo = pl.ds(pl.multiple_of(i * CHUNK, CHUNK), CHUNK)
+            hi = pl.ds(pl.multiple_of(HALF + i * CHUNK, CHUNK), CHUNK)
+            into[:, lo] = jnp.concatenate([at(lo), at(hi)], axis=0).astype(BF16)
+
+        pl.loop(0, HALF // CHUNK)(step)
+
+    fold_step(normed_at, fold_n)
     x_n = net.send("x", 1, fold_n, from_n)
+    fold_step(lambda cols: cot_ref[:, cols].astype(F32), fold_c)
+    x_c = net.send("x", 1, fold_c, from_c)
     arrive(u_1)
     u_z[z] = u_y[:, z]
     u_2 = net.ring("z", lambda d: u_y.at[:, net.coord("z", d)], lambda d: u_z.at[z])
-    x_c = net.send("x", 1, fold_c, from_c)
 
     def unfold(folded, received, full):
         def step(i):
@@ -144,28 +186,20 @@
         pl.loop(0, HALF // CHUNK)(step)
 
     a_cols, b_cols = pl.ds(0, HALF), pl.ds(HALF, HALF)
-
-    def gather_start(full):
-        own_a, own_b = full.at[z, y, :, a_cols], full.at[z, y, :, b_cols]
-        za = net.ring("z", lambda d: own_a, lambda d: own_a)
-        yb = net.ring("y", lambda d: own_b, lambda d: own_b)
-        return za, yb
-
-    def gather_on(full, za, yb):
-        arrive(za)
-        part = full.at[:, y, :, a_cols]
-        out = net.ring("y", lambda d: part, lambda d: part)
-        arrive(yb)
-        part_b = full.at[z, :, :, b_cols]
-        return out + net.ring("z", lambda d: part_b, lambda d: part_b)
-
+    gather_n = [Gather(net, n_all, "z", "y", 0), Gather(net, n_all, "y", "z", HALF)]
+    gather_c = [Gather(net, c_all, "z", "y", 0), Gather(net, c_all, "y", "z", HALF)]
+    x_n.wait_recv()
+    unfold(fold_n, from_n, n_all)
+    for half in gather_n:
+        half.start()
 
     arrive(u_2)
     u_x[x] = u_z[:, :, x]
     u_3 = net.send("x", 1, u_z.at[:, :, 1 - x], u_x.at[x])
-    x_n.wait_recv()
-    unfold(fold_n, from_n, n_all)
-    n_1 = gather_start(n_all)
+    x_c.wait_recv()
+    unfold(fold_c, from_c, c_all)
+    for half in gather_n:
+        half.middle()
 
     u_3.wait_recv()
     units = u_x[...].reshape(256, HD).astype(BF16)
@@ -176,6 +210,8 @@
         pick = jnp.where(col == at + 4 * half, 1.0, 0.0).astype(BF16)
         feat_all[s, :, half * HD : (half + 1) * HD] = dot(pick, units).astype(BF16)
     f_0 = net.ring("s", lambda d: feat_all.at[s], lambda d: feat_all.at[s])
+    for half in gather_n:
+        half.spread()
     arrive(f_0)
 
     loads[0].wait()
@@ -184,61 +220,70 @@
         cols = pl.ds(pl.multiple_of(h * HD, HD), HD)
         vcols = pl.ds(pl.multiple_of(1024 + h * HD, HD), HD)
         feats = feat_all[...].reshape(512, 256)
-        pk[h // 2, h % 2] = dot(feats, wkv[:, cols]).astype(BF16).reshape(4, 128, HD)
+        pk[h // 2, h % 2] = dot(feats, wkv[:, cols]).reshape(4, 128, HD)
         pv[h // 2, h % 2] = dot(feats, wkv[:, vcols]).astype(BF16).reshape(4, 128, HD)
 
     pl.loop(0, 8)(kv_step)
-    k_1 = net.ring("y", lambda d: pk.at[:, :, net.coord("y", d)], lambda d: k1.at[d - 1])
-    v_1 = net.ring("z", lambda d: pv.at[net.coord("z", d)], lambda d: v1.at[d - 1])
-
-    arrive(k_1)
-    for a in range(4):
+
+    def term(part, axis, at, rows):
+        return part.at[:, :, at, rows] if axis == "y" else part.at[at, :, :, rows]
+
+    chains = []
+    for part, y_buf, z_buf in ((pk, k_y, k_z), (pv, v_y, v_z)):
+        for n, (axis, buf) in enumerate((("y", y_buf), ("z", z_buf))):
+            rows = pl.ds(64 * n, 64)
+            copies = net.ring(
+                axis,
+                lambda d: term(part, axis, net.coord(axis, d), rows),
+                lambda d: buf.at[d - 1],
+            )
+            chains.append([part, axis, n, rows, buf, copies])
+    for half in gather_n:
+        half.forward()
+    for half in gather_c:
+        half.start()
+    for c, (part, axis, n, rows, buf, copies) in enumerate(chains):
+        arrive(copies)
+        for a in range(4):
+            for b in range(2):
+                at = (a, b) if axis == "y" else (b, a)
+                own = part[a, b, y, rows] if axis == "y" else part[z, b, a, rows]
+                total = own.astype(F32)
+                for d in range(3):
+                    total += buf[(d, *at)].astype(F32)
+                kv_1[(c, a, b)] = total
+        chains[c][5] = net.ring(
+            "z" if axis == "y" else "y",
+            lambda d: kv_1.at[c, net.coord("z" if axis == "y" else "y", d)],
+            lambda d: kv_2.at[c, d - 1],
+        )
+    for half in gather_c:
+        half.middle()
+    kv_x = []
+    for c, (part, axis, n, rows, buf, copies) in enumerate(chains):
+        arrive(copies)
+        mine = z if axis == "y" else y
         for b in range(2):
-            total = pk[a, b, y].astype(F32)
+            total = kv_1[c, mine, b]
             for d in range(3):
-                total += k1[d, a, b].astype(F32)
-            ks1[a, b] = total
-    k_2 = net.ring("z", lambda d: ks1.at[net.coord("z", d)], lambda d: k2.at[d - 1])
-    arrive(v_1)
-    for b in range(2):
-        for c in range(4):
-            total = pv[z, b, c].astype(F32)
-            for d in range(3):
-                total += v1[d, b, c].astype(F32)
-            vs1[b, c] = total
-    v_2 = net.ring("y", lambda d: vs1.at[:, net.coord("y", d)], lambda d: v2.at[d - 1])
-
-    n_2 = gather_on(n_all, *n_1)
-    x_c.wait_recv()
-    unfold(fold_c, from_c, c_all)
-
-    arrive(k_2)
-    arrive(v_2)
-    for b in range(2):
-        total = ks1[z, b]
-        vtotal = vs1[b, y]
-        for d in range(3):
-            total += k2[d, b]
-            vtotal += v2[d, b]
-        ks2[b] = total
-        vs2[b] = vtotal
-    k_x = net.send("x", 1, ks2.at[1 - x], kx)
-    v_x = net.send("x", 1, vs2.at[1 - x], vx)
-    c_1 = gather_start(c_all)
-    k_x.wait_recv()
-    v_x.wait_recv()
-    keys[y] = (ks2[x] + kx[...]).astype(BF16)
-    values[y] = (vs2[x] + vx[...]).astype(BF16)
+                total += kv_2[c, d, b]
+            kv_3[c, b] = total
+        kv_x.append(net.send("x", 1, kv_3.at[c, 1 - x], kv_4.at[c]))
+    for half in gather_c:
+        half.spread()
+    for c, (part, axis, n, rows, buf, copies) in enumerate(chains):
+        kv_x[c].wait_recv()
+        (keys if c < 2 else values)[y, 64 * n : 64 * n + 64] = (kv_3[c, x] + kv_4[c]).astype(BF16)
     k_3 = net.ring("y", lambda d: keys.at[y], lambda d: keys.at[y])
     v_3 = net.ring("y", lambda d: values.at[y], lambda d: values.at[y])
-
-    arrive(n_2)
+    feat_t[...] = feat_all[...].reshape(512, 256).astype(F32).T.astype(BF16)
+
+    for half in gather_n:
+        half.end()
     stores = []
     copy = pltpu.make_async_copy(n_all, n_out, local_sems.at[3])
     copy.start()
     stores.append(copy)
-    c_2 = gather_on(c_all, *c_1)
-
     loads[1].wait()
 
     def query_step(i, acc):
@@ -247,6 +292,8 @@
 
     query = lax.fori_loop(0, D // CHUNK, query_step, jnp.zeros((TOK, 256), F32)).astype(BF16)
 
+    for half in gather_c:
+        half.forward()
     arrive(k_3)
     arrive(v_3)
     key = keys[...].reshape(512, HD)
@@ -264,7 +311,8 @@
         weights.append(prob.astype(BF16))
         attn_out[:, j * HD : (j + 1) * HD] = dot(weights[j], value).astype(BF16)
 
-    arrive(c_2)
+    for half in gather_c:
+        half.end()
     copy = pltpu.make_async_copy(c_all, c_out, local_sems.at[4])
     copy.start()
     stores.append(copy)
@@ -297,12 +345,54 @@
         normed = n_all[:, :, :, cols].reshape(TOK, CHUNK).astype(F32)
         gain_part[:, cols] = jnp.sum(part * normed, axis=0, keepdims=True) / gain_ref[:, cols]
 
+    def line(axis, d, cols):
+        at = net.coord(axis, d)
+        return pd.at[:, at, :, cols] if axis == "y" else pd.at[at, :, :, cols]
+
+    def reduce_start(axis, start, via, near):
+        subs = (pl.ds(start, QUART), pl.ds(start + QUART, QUART))
+        far = [
+            net.send(axis, d, line(axis, 2, subs[n]), via.at[n]) for n, d in enumerate((1, 3))
+        ]
+        direct = [
+            net.send(axis, d, line(axis, d, subs[1 - n]), near.at[n, :, :, pl.ds((1 - n) * QUART, QUART)])
+            for n, d in enumerate((1, 3))
+        ]
+        return far, direct
+
+    def reduce_on(axis, start, via, relay, near, far):
+        out = []
+        for n, d in enumerate((1, 3)):
+            far[n].wait_recv()
+            at = net.coord(axis, d)
+
+            def step(i):
+                cols = pl.ds(pl.multiple_of(i * CHUNK, CHUNK), CHUNK)
+                own = pl.ds(pl.multiple_of(start + n * QUART + i * CHUNK, CHUNK), CHUNK)
+                mine = pd[:, at, :, own] if axis == "y" else pd[at, :, :, own]
+                relay[n, :, :, cols] = (mine.astype(F32) + via[n, :, :, cols].astype(F32)).astype(BF16)
+
+            pl.loop(0, QUART // CHUNK)(step)
+            out.append(net.send(axis, d, relay.at[n], near.at[n, :, :, pl.ds(n * QUART, QUART)]))
+        return out
+
+    def reduce_end(axis, start, near, copies, into):
+        arrive(copies)
+
+        def step(i):
+            cols = pl.ds(pl.multiple_of(i * CHUNK, CHUNK), CHUNK)
+            own = pl.ds(pl.multiple_of(start + i * CHUNK, CHUNK), CHUNK)
+            total = (pd[:, y, :, own] if axis == "y" else pd[z, :, :, own]).astype(F32)
+            into[:, :, cols] = (
+                total + near[0, :, :, cols].astype(F32) + near[1, :, :, cols].astype(F32)
+            ).astype(BF16)
+
+        pl.loop(0, HALF // CHUNK)(step)
+
     columns(0, HALF, d_normed_step)
-    da_1 = net.ring(
-        "y", lambda d: pd.at[:, net.coord("y", d), :, a_cols], lambda d: da1.at[d - 1]
-    )
+    da_far, da_near = reduce_start("y", 0, via_a, near_a)
     columns(HALF, D, d_normed_step)
-    db_1 = net.ring("z", lambda d: pd.at[net.coord("z", d), :, :, b_cols], lambda d: db1.at[d - 1])
+    db_far, db_near = reduce_start("z", HALF, via_b, near_b)
     for i in range(8):
         gz[z, i : i + 1, :] = gain_part[:, i * 1024 : (i + 1) * 1024]
     g_1 = net.ring("z", lambda d: gz.at[z], lambda d: gz.at[z])
@@ -324,54 +414,42 @@
     pair_k, pair_v = dkg.at[z, :, y], dvg.at[z, :, y]
     dk_3 = net.ring("z", lambda d: pair_k, lambda d: pair_k)
     dv_3 = net.ring("y", lambda d: pair_v, lambda d: pair_v)
-    arrive(g_1)
-    gy[y] = (gz[0] + gz[1]) + (gz[2] + gz[3])
-    g_2 = net.ring("y", lambda d: gy.at[y], lambda d: gy.at[y])
+    da_near += reduce_on("y", 0, via_a, relay_a, near_a, da_far)
     arrive(dk_3)
     line_k = dkg.at[:, :, y]
     dk_4 = net.ring("y", lambda d: line_k, lambda d: line_k)
     arrive(dv_3)
     line_v = dvg.at[z]
     dv_4 = net.ring("z", lambda d: line_v, lambda d: line_v)
-
+    db_near += reduce_on("z", HALF, via_b, relay_b, near_b, db_far)
+    arrive(g_1)
+    gy[y] = (gz[0] + gz[1]) + (gz[2] + gz[3])
+    g_2 = net.ring("y", lambda d: gy.at[y], lambda d: gy.at[y])
+
+    reduce_end("y", 0, near_a, da_near, sa1)
+    da_2 = net.ring("z", lambda d: sa1.at[net.coord("z", d)], lambda d: da2.at[d - 1])
+    reduce_end("z", HALF, near_b, db_near, sb1)
+    db_2 = net.ring("y", lambda d: sb1.at[net.coord("y", d)], lambda d: db2.at[d - 1])
     arrive(g_2)
     gx2[x] = (gy[0] + gy[1]) + (gy[2] + gy[3])
     g_3 = net.send("x", 1, gx2.at[x], gx2.at[x])
-    arrive(da_1)
-
-    def sum_a(i):
-        cols = pl.ds(pl.multiple_of(i * CHUNK, CHUNK), CHUNK)
-        total = pd[:, y, :, cols].astype(F32)
-        for d in range(3):
-            total += da1[d, :, :, cols].astype(F32)
-        sa1[:, :, cols] = total.astype(BF16)
-
-    pl.loop(0, HALF // CHUNK)(sum_a)
-    da_2 = net.ring("z", lambda d: sa1.at[net.coord("z", d)], lambda d: da2.at[d - 1])
-    arrive(db_1)
-
-    def sum_b(i):
-        cols = pl.ds(pl.multiple_of(i * CHUNK, CHUNK), CHUNK)
-        far = pl.ds(pl.multiple_of(HALF + i * CHUNK, CHUNK), CHUNK)
-        total = pd[z, :, :, far].astype(F32)
-        for d in range(3):
-            total += db1[d, :, :, cols].astype(F32)
-        sb1[:, :, cols] = total.astype(BF16)
-
-    pl.loop(0, HALF // CHUNK)(sum_b)
-    db_2 = net.ring("y", lambda d: sb1.at[net.coord("y", d)], lambda d: db2.at[d - 1])
 
     arrive(dk_4)
     arrive(dv_4)
-    feats = feat_all[...].reshape(512, 256)
     d_feats = jnp.zeros((512, 256), F32)
     for h in range(8):
+        both = jnp.concatenate(
+            [full[h // 2, h % 2].reshape(512, HD) for full in (dkg, dvg)], axis=1
+        )
+        weights_h = jnp.concatenate(
+            [wkv[:, at : at + HD] for at in (h * HD, 1024 + h * HD)], axis=1
+        )
+        d_feats += dot(both, weights_h, NT)
+    df[...] = d_feats.astype(BF16).reshape(4, 128, 256)
+    f_1 = net.ring("s", lambda d: df.at[net.coord("s", d)], lambda d: dfr.at[d - 1])
+    for h in range(8):
         for at, full in ((h * HD, dkg), (1024 + h * HD, dvg)):
-            grad = full[h // 2, h % 2].reshape(512, HD)
-            gkv_out[:, at : at + HD] = dot(feats, grad, TN).astype(BF16)
-            d_feats += dot(grad, wkv[:, at : at + HD], NT)
-    df[...] = d_feats.reshape(4, 128, 256)
-    f_1 = net.ring("s", lambda d: df.at[net.coord("s", d)], lambda d: dfr.at[d - 1])
+            gkv_out[:, at : at + HD] = dot(feat_t[...], full[h // 2, h % 2].reshape(512, HD)).astype(BF16)
 
     arrive(da_2)
     arrive(db_2)
@@ -393,9 +471,9 @@
     d_x = net.send("x", 1, fold_d, from_d)
 
     arrive(f_1)
-    img = df[s]
+    img = df[s].astype(F32)
     for d in range(3):
-        img += dfr[d]
+        img += dfr[d].astype(F32)
     img_s[...] = img.reshape(4, 32, 256)
     img_z[z] = img_s[z]
     f_2 = net.ring("z", lambda d: img_s.at[net.coord("z", d)], lambda d: img_z.at[z])
@@ -454,21 +532,19 @@
             b(4, 4, 16, D), b(4, 4, 16, D), b(D, 256), b(256, D), b(256, 2048),
             f(4, 4, 2, 8, HD), f(4, 4, 2, 8, HD), f(2, 4, 4, 8, HD), b(4, 128, 256),
             b(16, HALF), b(16, HALF), b(16, HALF), b(16, HALF),
-            b(4, 2, 4, 128, HD), b(4, 2, 4, 128, HD),
-            b(3, 4, 2, 128, HD), b(3, 2, 4, 128, HD),
-            f(4, 2, 128, HD), f(2, 4, 128, HD),
-            f(3, 2, 128, HD), f(3, 2, 128, HD),
-            f(2, 128, HD), f(2, 128, HD),
-            f(128, HD), f(128, HD),
+            b(256, 512), f(4, 2, 4, 128, HD), b(4, 2, 4, 128, HD),
+            f(3, 4, 2, 64, HD), f(3, 2, 4, 64, HD), b(3, 4, 2, 64, HD), b(3, 2, 4, 64, HD),
+            f(4, 4, 2, 64, HD), f(4, 3, 2, 64, HD), f(4, 2, 64, HD), f(4, 64, HD),
             b(4, 128, HD), b(4, 128, HD),
             b(4, 128, HD), b(4, 128, HD), b(3, 128, HD), b(3, 128, HD),
             b(4, 2, 4, 128, HD), b(4, 2, 4, 128, HD),
             b(4, 4, 16, D),
-            b(3, 4, 16, HALF), b(3, 4, 16, HALF),
+            b(2, 4, 16, QUART), b(2, 4, 16, QUART), b(2, 4, 16, QUART), b(2, 4, 16, QUART),
+            b(2, 4, 16, HALF), b(2, 4, 16, HALF),
             b(4, 16, HALF), b(4, 16, HALF),
             b(3, 16, HALF), b(3, 16, HALF),
             f(16, HALF), b(16, HALF), b(16, HALF),
-            f(4, 128, 256), f(3, 128, 256),
+            b(4, 128, 256), b(3, 128, 256),
             f(4, 32, 256), f(4, 32, 256), f(2, 4, 16, 256), f(4, 2, 4, 8, 256),
             f(1, D), f(4, 8, 1024), f(4, 8, 1024), f(2, 8, 1024),
             pltpu.SemaphoreType.DMA((NSEM,)),
@@ -512,7 +588,7 @@
             pl.BlockSpec((256, width), lambda i: (0, i)),
             pl.BlockSpec((VCOLS, kv_width), lambda i: (0, i)),
         ),
-        compiler_params=pltpu.CompilerParams(vmem_limit_bytes=32 * 1024 * 1024),
+        compiler_params=pltpu.CompilerParams(vmem_limit_bytes=62 * 1024 * 1024),
         name="weight_grads",
     )(normed, cotangent, attn, d_query, grad_kv)
 

time: 193 us -> 168 us (0.87)
  Pallas kernels: 180 us -> 162 us
  local copies, waits for them, and re-layouts: 11.9 us -> 4.51 us
    pallas_call x1, Pallas kernels: 173 us -> 151 us  [run_layer(): pl.pallas_call(layer_kernel, out_shape=(shape((4, 4, 16, D), BF16), shape...]
    unnamed x17 -> x7, local copies, waits for them, and re-layouts: 10.1 us -> 2.72 us
    pallas_call x1, Pallas kernels: 6.92 us -> 11.2 us  [weight_grads(): pl.pallas_call(weight_kernel, grid=(steps,), out_shape=(shape((D, 256), B...]
where the time goes in v3:
time: 168 us; the launch traced here: 167 us
  Pallas kernels  162 us (96%)
  local copies, waits for them, and re-layouts  4.51 us (3%)
    pallas_call x1, Pallas kernels, run_layer(): pl.pallas_call(layer_kernel, out_shape=(shape((4, 4, 16, D), BF16), shape...  151 us
    pallas_call x1, Pallas kernels, weight_grads(): pl.pallas_call(weight_kernel, grid=(steps,), out_shape=(shape((D, 256), B...  11.2 us

profile of v3, /device:TPU:0, one launch (start us, length us, event | category | flops | bytes accessed | tf_op | source)
XLA Modules:
  0.0 167.1 jit_solution(14369172381103489563)
XLA Ops:
  0.6 1.0 reshape.28
  1.6 0.1 reshape.37
  1.7 0.7 copy.14
  2.5 150.7 %layer.1 = (bf16[4,4,16,8192]{3,2,1,0:T(8,128)(2,1)}, bf16[4,4,16,8192]{3,2,1,0:T(8,128)(2,1)}, bf16[256,256]{1,0:T(8,128)(2,1)}, bf16[256,256]{1,0:T(8,128)(2,1...) custom-call(bf16[8,8192]{1,0:T(8,128)(2,1)} %bitcast.25, ...), custom_call_target="tpu_custom_call" | custom-call | flops 6000000000 | bytes 20971520 | tf_op jit(solution)/shard_map/layer/pallas_call | solution.py:517
  153.2 1.4 copy.15
  154.6 0.0 copy-start
  154.6 0.0 copy-start.1
  154.6 11.2 %weight_grads.1 = (bf16[8192,256]{1,0:T(8,128)(2,1)}, bf16[256,8192]{1,0:T(8,128)(2,1)}, bf16[240,2048]{1,0:T(8,128)(2,1)}) custom-call(bf16[4,4,16,8192]{3,2,1,0:T(8,128)(2,1)} %get-tuple-element.19.n_ref, bf16[4,4,16,8192]{3,2,1,0:T(8,128)(2,1)} %get-tuple-element.20.c_ref, bf16[256,256]{1,0:T(8,128)(2,1)} %get-tuple-element.21.attn_ref, ...), custom_call_target="tpu_custom_call" | custom-call | tf_op jit(solution)/shard_map/weight_grads/pallas_call | solution.py:577
  165.8 0.0 copy-done
  165.8 0.7 copy.18
  166.5 0.0 copy-done.1
  166.5 0.6 copy.19
  (1 shorter events, 0.0 us)
Async XLA Ops:
  154.6 11.2 %copy-start = (bf16[8,8192]{1,0:T(8,128)(2,1)S(1)}, bf16[8,8192]{1,0:T(8,128)(2,1)}, u32[]{:S(2)}) copy-start(bf16[8,8192]{1,0:T(8,128)(2,1)} %get-tuple-element.17) | copy-start | bytes 393220
  154.6 11.9 %copy-start.1 = (f32[4,7680]{1,0:T(4,128)S(1)}, f32[4,7680]{1,0:T(4,128)}, u32[]{:S(2)}) copy-start(f32[4,7680]{1,0:T(4,128)} %get-tuple-element.39) | copy-start | bytes 368644

commit v4 on v3

--- a/solution.py
+++ b/solution.py
@@ -16,7 +16,7 @@
 HD = 128
 VCOLS = 240
 SCALE = HD ** (-0.5)
-NSEM = 192
+NSEM = 224
 
 NT = (((1,), (1,)), ((), ()))
 TN = (((0,), (0,)), ((), ()))
@@ -49,7 +49,7 @@
         peers = [(a, d) for a in ("z", "y", "s") for d in (1, 2, 3)] + [("x", 1)]
         for a, d in peers:
             pl.semaphore_signal(sem, inc=1, device_id=self.peer(a, d), device_id_type=MESH)
-        pl.semaphore_wait(sem, len(peers))
+        return lambda: pl.semaphore_wait(sem, len(peers))
 
     def send(self, axis, d, src, dst):
         at = len(self.copies)
@@ -69,6 +69,7 @@
         return [self.send(axis, d, src(d), dst(d)) for d in (1, 3, 2)]
 
     def finish(self):
+        assert len(self.copies) <= NSEM
         for copy in self.copies:
             copy.wait_send()
 
@@ -79,14 +80,14 @@
 
 
 class Gather:
-    def __init__(self, net, full, first, second, start):
-        self.net, self.full, self.first, self.second = net, full, first, second
-        self.cols = pl.ds(start, HALF)
-        self.sub = (pl.ds(start, QUART), pl.ds(start + QUART, QUART))
+    def __init__(self, net, at, first, second, start, size):
+        self.net, self.at, self.first, self.second = net, at, first, second
+        self.cols = pl.ds(start, size)
+        self.sub = (pl.ds(start, size // 2), pl.ds(start + size // 2, size // 2))
 
     def block(self, i, j, cols):
         i, j = self.net.coord(self.first, i), self.net.coord(self.second, j)
-        return self.full.at[i, j, :, cols] if self.first == "z" else self.full.at[j, i, :, cols]
+        return self.at(i, j, cols) if self.first == "z" else self.at(j, i, cols)
 
     def push(self, axis, d, i, j, cols):
         block = self.block(i, j, cols)
@@ -127,10 +128,10 @@
 def layer_kernel(
     tok_ref, cot_ref, gain_ref, vis_ref, unit_ref, wq_hbm, wo_hbm, wkv_hbm,
     n_out, c_out, attn_out, dq_out, gkv_out, gx_out, gg_out, gi_out,
-    n_all, c_all, wq, wo, wkv,
+    n_all, c_all, n_t, wq, wo, wkv,
     u_y, u_z, u_x, feat_all,
     fold_n, fold_c, from_n, from_c,
-    feat_t, pk, pv, k_y, k_z, v_y, v_z, kv_1, kv_2, kv_3, kv_4, keys, values,
+    feat_t, pk, pv, kx, ks0, ks1, ks2, ks3, v_y, v_z, vs1, vs2, vs3, vx, keys, values,
     dk, dv, rk, rv, dkg, dvg,
     pd, via_a, via_b, relay_a, relay_b, near_a, near_b, sa1, sb1, da2, db2, own_d, fold_d, from_d,
     df, dfr, img_s, img_z, img_x, gi_all, gain_part, gz, gy, gx2,
@@ -138,17 +139,13 @@
 ):
     net = Links(send_sems, recv_sems)
     s, z, x, y = net.s, net.z, net.x, net.y
+    ready = net.barrier()
     loads = []
     wkv[VCOLS:, :] = jnp.zeros((256 - VCOLS, 2048), BF16)
     for i, (src, dst) in enumerate(((wkv_hbm, wkv.at[:VCOLS]), (wq_hbm, wq), (wo_hbm, wo))):
         copy = pltpu.make_async_copy(src, dst, local_sems.at[i])
         copy.start()
         loads.append(copy)
-    net.barrier()
-
-    u_y[y] = unit_ref[:, :, y]
-    u_1 = net.ring("y", lambda d: unit_ref.at[:, :, net.coord("y", d)], lambda d: u_y.at[y])
-
     xf = tok_ref[...].astype(F32)
     rinv = lax.rsqrt(jnp.mean(xf * xf, axis=-1, keepdims=True) + 1e-05)
 
@@ -164,7 +161,10 @@
         pl.loop(0, HALF // CHUNK)(step)
 
     fold_step(normed_at, fold_n)
+    ready()
     x_n = net.send("x", 1, fold_n, from_n)
+    u_y[y] = unit_ref[:, :, y]
+    u_1 = net.ring("y", lambda d: unit_ref.at[:, :, net.coord("y", d)], lambda d: u_y.at[y])
     fold_step(lambda cols: cot_ref[:, cols].astype(F32), fold_c)
     x_c = net.send("x", 1, fold_c, from_c)
     arrive(u_1)
@@ -186,8 +186,11 @@
         pl.loop(0, HALF // CHUNK)(step)
 
     a_cols, b_cols = pl.ds(0, HALF), pl.ds(HALF, HALF)
-    gather_n = [Gather(net, n_all, "z", "y", 0), Gather(net, n_all, "y", "z", HALF)]
-    gather_c = [Gather(net, c_all, "z", "y", 0), Gather(net, c_all, "y", "z", HALF)]
+    def gathers(full):
+        at = lambda i, j, cols: full.at[i, j, :, cols]
+        return [Gather(net, at, "z", "y", 0, HALF), Gather(net, at, "y", "z", HALF, HALF)]
+
+    gather_n, gather_c = gathers(n_all), gathers(c_all)
     x_n.wait_recv()
     unfold(fold_n, from_n, n_all)
     for half in gather_n:
@@ -225,65 +228,83 @@
 
     pl.loop(0, 8)(kv_step)
 
-    def term(part, axis, at, rows):
-        return part.at[:, :, at, rows] if axis == "y" else part.at[at, :, :, rows]
-
-    chains = []
-    for part, y_buf, z_buf in ((pk, k_y, k_z), (pv, v_y, v_z)):
-        for n, (axis, buf) in enumerate((("y", y_buf), ("z", z_buf))):
-            rows = pl.ds(64 * n, 64)
-            copies = net.ring(
-                axis,
-                lambda d: term(part, axis, net.coord(axis, d), rows),
-                lambda d: buf.at[d - 1],
-            )
-            chains.append([part, axis, n, rows, buf, copies])
+    axes = (("y", "z"), ("z", "y"))
+    halves = [pl.ds(0, 64), pl.ds(64, 64)]
+
+    def along(n, level, ref, d):
+        axis = axes[n][level]
+        at = net.coord(axis, d)
+        return ref.at[:, at] if level == 0 and n == 0 else ref.at[at]
+
+    k_x = [net.send("x", 1, pk.at[:, 1 - x, :, rows], kx.at[n]) for n, rows in enumerate(halves)]
+    v_1 = [
+        net.ring("y", lambda d: pv.at[:, :, net.coord("y", d), halves[0]], lambda d: v_y.at[d - 1]),
+        net.ring("z", lambda d: pv.at[net.coord("z", d), :, :, halves[1]], lambda d: v_z.at[d - 1]),
+    ]
     for half in gather_n:
         half.forward()
     for half in gather_c:
         half.start()
-    for c, (part, axis, n, rows, buf, copies) in enumerate(chains):
-        arrive(copies)
+
+    v_2 = []
+    for n in range(2):
+        arrive(v_1[n])
         for a in range(4):
             for b in range(2):
-                at = (a, b) if axis == "y" else (b, a)
-                own = part[a, b, y, rows] if axis == "y" else part[z, b, a, rows]
-                total = own.astype(F32)
+                total = (pv[a, b, y, halves[0]] if n == 0 else pv[z, b, a, halves[1]]).astype(F32)
                 for d in range(3):
-                    total += buf[(d, *at)].astype(F32)
-                kv_1[(c, a, b)] = total
-        chains[c][5] = net.ring(
-            "z" if axis == "y" else "y",
-            lambda d: kv_1.at[c, net.coord("z" if axis == "y" else "y", d)],
-            lambda d: kv_2.at[c, d - 1],
+                    total += (v_y[d, a, b] if n == 0 else v_z[d, b, a]).astype(F32)
+                vs1[n, a, b] = total
+        v_2.append(
+            net.ring(axes[n][1], lambda d: along(n, 1, vs1.at[n], d), lambda d: vs2.at[n, d - 1])
         )
     for half in gather_c:
         half.middle()
-    kv_x = []
-    for c, (part, axis, n, rows, buf, copies) in enumerate(chains):
-        arrive(copies)
-        mine = z if axis == "y" else y
+    k_2 = []
+    for n, rows in enumerate(halves):
+        k_x[n].wait_recv()
+        for a in range(4):
+            ks0[n, a] = pk[a, x, :, rows] + kx[n, a]
+        k_2.append(
+            net.ring(axes[n][0], lambda d: along(n, 0, ks0.at[n], d), lambda d: ks1.at[n, d - 1])
+        )
+    v_x = []
+    for n in range(2):
+        arrive(v_2[n])
+        mine = net.coord(axes[n][1], 0)
         for b in range(2):
-            total = kv_1[c, mine, b]
+            total = vs1[n, mine, b]
             for d in range(3):
-                total += kv_2[c, d, b]
-            kv_3[c, b] = total
-        kv_x.append(net.send("x", 1, kv_3.at[c, 1 - x], kv_4.at[c]))
+                total += vs2[n, d, b]
+            vs3[n, b] = total
+        v_x.append(net.send("x", 1, vs3.at[n, 1 - x], vx.at[n]))
     for half in gather_c:
         half.spread()
-    for c, (part, axis, n, rows, buf, copies) in enumerate(chains):
-        kv_x[c].wait_recv()
-        (keys if c < 2 else values)[y, 64 * n : 64 * n + 64] = (kv_3[c, x] + kv_4[c]).astype(BF16)
+    k_3 = []
+    for n in range(2):
+        arrive(k_2[n])
+        for a in range(4):
+            total = ks0[n, a, y] if n == 0 else ks0[n, z, a]
+            for d in range(3):
+                total += ks1[n, d, a]
+            ks2[n, a] = total
+        k_3.append(
+            net.ring(axes[n][1], lambda d: along(n, 1, ks2.at[n], d), lambda d: ks3.at[n, d - 1])
+        )
+    for n in range(2):
+        v_x[n].wait_recv()
+        values[y, 64 * n : 64 * n + 64] = (vs3[n, x] + vx[n]).astype(BF16)
+    v_3 = net.ring("y", lambda d: values.at[y], lambda d: values.at[y])
+    for n in range(2):
+        arrive(k_3[n])
+        total = ks2[n, net.coord(axes[n][1], 0)]
+        for d in range(3):
+            total += ks3[n, d]
+        keys[y, 64 * n : 64 * n + 64] = total.astype(BF16)
     k_3 = net.ring("y", lambda d: keys.at[y], lambda d: keys.at[y])
-    v_3 = net.ring("y", lambda d: values.at[y], lambda d: values.at[y])
-    feat_t[...] = feat_all[...].reshape(512, 256).astype(F32).T.astype(BF16)
 
     for half in gather_n:
         half.end()
-    stores = []
-    copy = pltpu.make_async_copy(n_all, n_out, local_sems.at[3])
-    copy.start()
-    stores.append(copy)
     loads[1].wait()
 
     def query_step(i, acc):
@@ -294,6 +315,7 @@
 
     for half in gather_c:
         half.forward()
+    stores = []
     arrive(k_3)
     arrive(v_3)
     key = keys[...].reshape(512, HD)
@@ -309,7 +331,8 @@
         prob = expo / jnp.sum(expo, axis=-1, keepdims=True)
         probs.append(prob)
         weights.append(prob.astype(BF16))
-        attn_out[:, j * HD : (j + 1) * HD] = dot(weights[j], value).astype(BF16)
+        attn = dot(weights[j], value).astype(BF16)
+        attn_out[j * HD : (j + 1) * HD, :] = attn.astype(F32).T.astype(BF16)
 
     for half in gather_c:
         half.end()
@@ -342,6 +365,9 @@
     def d_normed_step(cols):
         part = dot(dq_out[...], wq[cols, :], NT)
         pd[:, :, :, cols] = part.astype(BF16).reshape(4, 4, 16, CHUNK)
+
+    def gain_step(cols):
+        part = pd[:, :, :, cols].reshape(TOK, CHUNK).astype(F32)
         normed = n_all[:, :, :, cols].reshape(TOK, CHUNK).astype(F32)
         gain_part[:, cols] = jnp.sum(part * normed, axis=0, keepdims=True) / gain_ref[:, cols]
 
@@ -349,16 +375,18 @@
         at = net.coord(axis, d)
         return pd.at[:, at, :, cols] if axis == "y" else pd.at[at, :, :, cols]
 
-    def reduce_start(axis, start, via, near):
-        subs = (pl.ds(start, QUART), pl.ds(start + QUART, QUART))
-        far = [
-            net.send(axis, d, line(axis, 2, subs[n]), via.at[n]) for n, d in enumerate((1, 3))
-        ]
-        direct = [
-            net.send(axis, d, line(axis, d, subs[1 - n]), near.at[n, :, :, pl.ds((1 - n) * QUART, QUART)])
+    def reduce_far(axis, start, via):
+        return [
+            net.send(axis, d, line(axis, 2, pl.ds(start + n * QUART, QUART)), via.at[n])
             for n, d in enumerate((1, 3))
         ]
-        return far, direct
+
+    def reduce_near(axis, start, near):
+        out = []
+        for n, d in enumerate((1, 3)):
+            block = line(axis, d, pl.ds(start + (1 - n) * QUART, QUART))
+            out.append(net.send(axis, d, block, near.at[n, :, :, pl.ds((1 - n) * QUART, QUART)]))
+        return out
 
     def reduce_on(axis, start, via, relay, near, far):
         out = []
@@ -390,13 +418,9 @@
         pl.loop(0, HALF // CHUNK)(step)
 
     columns(0, HALF, d_normed_step)
-    da_far, da_near = reduce_start("y", 0, via_a, near_a)
+    da_far = reduce_far("y", 0, via_a)
     columns(HALF, D, d_normed_step)
-    db_far, db_near = reduce_start("z", HALF, via_b, near_b)
-    for i in range(8):
-        gz[z, i : i + 1, :] = gain_part[:, i * 1024 : (i + 1) * 1024]
-    g_1 = net.ring("z", lambda d: gz.at[z], lambda d: gz.at[z])
-
+    db_far = reduce_far("z", HALF, via_b)
     arrive(dk_1)
     arrive(dv_1)
     total = dk[y].astype(F32)
@@ -409,33 +433,45 @@
     mine_k, mine_v = dkg.at[z, x, y], dvg.at[z, x, y]
     dk_2 = net.send("x", 1, mine_k, mine_k)
     dv_2 = net.send("x", 1, mine_v, mine_v)
+    gather_d = [
+        Gather(net, lambda i, j, rows: dkg.at[i, :, j, rows], "z", "y", 0, HD),
+        Gather(net, lambda i, j, rows: dvg.at[i, :, j, rows], "y", "z", 0, HD),
+    ]
     dk_2.wait_recv()
     dv_2.wait_recv()
-    pair_k, pair_v = dkg.at[z, :, y], dvg.at[z, :, y]
-    dk_3 = net.ring("z", lambda d: pair_k, lambda d: pair_k)
-    dv_3 = net.ring("y", lambda d: pair_v, lambda d: pair_v)
-    da_near += reduce_on("y", 0, via_a, relay_a, near_a, da_far)
-    arrive(dk_3)
-    line_k = dkg.at[:, :, y]
-    dk_4 = net.ring("y", lambda d: line_k, lambda d: line_k)
-    arrive(dv_3)
-    line_v = dvg.at[z]
-    dv_4 = net.ring("z", lambda d: line_v, lambda d: line_v)
-    db_near += reduce_on("z", HALF, via_b, relay_b, near_b, db_far)
+    for part in gather_d:
+        part.start()
+    columns(0, D, gain_step)
+    for i in range(8):
+        gz[z, i : i + 1, :] = gain_part[:, i * 1024 : (i + 1) * 1024]
+    g_1 = net.ring("z", lambda d: gz.at[z], lambda d: gz.at[z])
+
+    for part in gather_d:
+        part.middle()
+    da_near = reduce_on("y", 0, via_a, relay_a, near_a, da_far)
+    for part in gather_d:
+        part.spread()
+    db_near = reduce_on("z", HALF, via_b, relay_b, near_b, db_far)
+    for part in gather_d:
+        part.forward()
+    da_near += reduce_near("y", 0, near_a)
+    db_near += reduce_near("z", HALF, near_b)
+    feat_t[...] = feat_all[...].reshape(512, 256).astype(F32).T.astype(BF16)
+
+    def turn_step(i):
+        cols = pl.ds(pl.multiple_of(i * CHUNK, CHUNK), CHUNK)
+        n_t[cols, :] = n_all[:, :, :, cols].reshape(TOK, CHUNK).astype(F32).T.astype(BF16)
+
+    pl.loop(0, D // CHUNK)(turn_step)
+    copy = pltpu.make_async_copy(n_t, n_out, local_sems.at[3])
+    copy.start()
+    stores.append(copy)
     arrive(g_1)
     gy[y] = (gz[0] + gz[1]) + (gz[2] + gz[3])
     g_2 = net.ring("y", lambda d: gy.at[y], lambda d: gy.at[y])
 
-    reduce_end("y", 0, near_a, da_near, sa1)
-    da_2 = net.ring("z", lambda d: sa1.at[net.coord("z", d)], lambda d: da2.at[d - 1])
-    reduce_end("z", HALF, near_b, db_near, sb1)
-    db_2 = net.ring("y", lambda d: sb1.at[net.coord("y", d)], lambda d: db2.at[d - 1])
-    arrive(g_2)
-    gx2[x] = (gy[0] + gy[1]) + (gy[2] + gy[3])
-    g_3 = net.send("x", 1, gx2.at[x], gx2.at[x])
-
-    arrive(dk_4)
-    arrive(dv_4)
+    for part in gather_d:
+        part.end()
     d_feats = jnp.zeros((512, 256), F32)
     for h in range(8):
         both = jnp.concatenate(
@@ -447,10 +483,28 @@
         d_feats += dot(both, weights_h, NT)
     df[...] = d_feats.astype(BF16).reshape(4, 128, 256)
     f_1 = net.ring("s", lambda d: df.at[net.coord("s", d)], lambda d: dfr.at[d - 1])
+    reduce_end("y", 0, near_a, da_near, sa1)
+    da_2 = net.ring("z", lambda d: sa1.at[net.coord("z", d)], lambda d: da2.at[d - 1])
+    reduce_end("z", HALF, near_b, db_near, sb1)
+    db_2 = net.ring("y", lambda d: sb1.at[net.coord("y", d)], lambda d: db2.at[d - 1])
+    arrive(f_1)
+    img = df[s].astype(F32)
+    for d in range(3):
+        img += dfr[d].astype(F32)
+    img_s[...] = img.reshape(4, 32, 256)
+    img_z[z] = img_s[z]
+    f_2 = net.ring("z", lambda d: img_s.at[net.coord("z", d)], lambda d: img_z.at[z])
     for h in range(8):
         for at, full in ((h * HD, dkg), (1024 + h * HD, dvg)):
             gkv_out[:, at : at + HD] = dot(feat_t[...], full[h // 2, h % 2].reshape(512, HD)).astype(BF16)
-
+    arrive(g_2)
+    gx2[x] = (gy[0] + gy[1]) + (gy[2] + gy[3])
+    g_3 = net.send("x", 1, gx2.at[x], gx2.at[x])
+
+    arrive(f_2)
+    img_x[x] = img_z[:, pl.ds(pl.multiple_of(x * 16, 16), 16), :]
+    far = pl.ds(pl.multiple_of((1 - x) * 16, 16), 16)
+    f_3 = net.send("x", 1, img_z.at[:, far], img_x.at[x])
     arrive(da_2)
     arrive(db_2)
 
@@ -470,16 +524,17 @@
     pl.loop(0, HALF // CHUNK)(sum_ab)
     d_x = net.send("x", 1, fold_d, from_d)
 
-    arrive(f_1)
-    img = df[s].astype(F32)
-    for d in range(3):
-        img += dfr[d].astype(F32)
-    img_s[...] = img.reshape(4, 32, 256)
-    img_z[z] = img_s[z]
-    f_2 = net.ring("z", lambda d: img_s.at[net.coord("z", d)], lambda d: img_z.at[z])
-
+    f_3.wait_recv()
+
+    def tile(d):
+        return pl.ds(pl.multiple_of((net.coord("y", d) // 2) * 8, 8), 8)
+
+    gi_all[y] = img_x[:, :, tile(0), :]
+    f_4 = net.ring("y", lambda d: img_x.at[:, :, tile(d)], lambda d: gi_all.at[y])
     g_3.wait_recv()
-    gg_out[...] = gx2[0] + gx2[1]
+    gain = gx2[0] + gx2[1]
+    for i in range(8):
+        gg_out[:, i * 1024 : (i + 1) * 1024] = gain[i : i + 1]
     d_x.wait_recv()
     both = own_d[...] + from_d[...].astype(F32)
     dn = jnp.concatenate([both[:8], both[8:]], axis=1)
@@ -488,17 +543,6 @@
     gx_out[...] = (
         rinv * scaled - xf * rinv * rinv * rinv * jnp.mean(xf * scaled, axis=-1, keepdims=True)
     ).astype(BF16)
-    arrive(f_2)
-    img_x[x] = img_z[:, pl.ds(pl.multiple_of(x * 16, 16), 16), :]
-    far = pl.ds(pl.multiple_of((1 - x) * 16, 16), 16)
-    f_3 = net.send("x", 1, img_z.at[:, far], img_x.at[x])
-    f_3.wait_recv()
-
-    def tile(d):
-        return pl.ds(pl.multiple_of((net.coord("y", d) // 2) * 8, 8), 8)
-
-    gi_all[y] = img_x[:, :, tile(0), :]
-    f_4 = net.ring("y", lambda d: img_x.at[:, :, tile(d)], lambda d: gi_all.at[y])
     arrive(f_4)
     for m in range(32):
         tile_m = gi_all[m % 4, (m // 4) % 2, m // 8]
@@ -517,24 +561,26 @@
     return pl.pallas_call(
         layer_kernel,
         out_shape=(
-            shape((4, 4, 16, D), BF16),
+            shape((D, 256), BF16),
             shape((4, 4, 16, D), BF16),
             shape((TOK, 256), BF16),
             shape((TOK, 256), BF16),
             shape((256, 2048), BF16),
             shape((8, D), BF16),
-            shape((8, 1024), F32),
+            shape((1, D), F32),
             shape((4, 32 * VCOLS), F32),
         ),
         in_specs=[vmem, vmem, vmem, smem, vmem, any_spec, any_spec, any_spec],
         out_specs=(any_spec, any_spec, vmem, vmem, vmem, vmem, vmem, vmem),
         scratch_shapes=[
-            b(4, 4, 16, D), b(4, 4, 16, D), b(D, 256), b(256, D), b(256, 2048),
+            b(4, 4, 16, D), b(4, 4, 16, D), b(D, 256), b(D, 256), b(256, D), b(256, 2048),
             f(4, 4, 2, 8, HD), f(4, 4, 2, 8, HD), f(2, 4, 4, 8, HD), b(4, 128, 256),
             b(16, HALF), b(16, HALF), b(16, HALF), b(16, HALF),
             b(256, 512), f(4, 2, 4, 128, HD), b(4, 2, 4, 128, HD),
-            f(3, 4, 2, 64, HD), f(3, 2, 4, 64, HD), b(3, 4, 2, 64, HD), b(3, 2, 4, 64, HD),
-            f(4, 4, 2, 64, HD), f(4, 3, 2, 64, HD), f(4, 2, 64, HD), f(4, 64, HD),
+            f(2, 4, 4, 64, HD), f(2, 4, 4, 64, HD), f(2, 3, 4, 64, HD),
+            f(2, 4, 64, HD), f(2, 3, 64, HD),
+            b(3, 4, 2, 64, HD), b(3, 2, 4, 64, HD), f(2, 4, 2, 64, HD), f(2, 3, 2, 64, HD),
+            f(2, 2, 64, HD), f(2, 64, HD),
             b(4, 128, HD), b(4, 128, HD),
             b(4, 128, HD), b(4, 128, HD), b(3, 128, HD), b(3, 128, HD),
             b(4, 2, 4, 128, HD), b(4, 2, 4, 128, HD),
@@ -561,19 +607,25 @@
     )(tokens, cotangent, gain_row, visible, units, w_q, w_o, w_kv)
 
 
-def weight_kernel(n_ref, c_ref, attn_ref, dq_ref, gkv_ref, gq_ref, go_ref, gk_ref):
-    width = n_ref.shape[-1]
-    gq_ref[...] = dot(n_ref[...].reshape(TOK, width), dq_ref[...], TN).astype(BF16)
-    go_ref[...] = dot(attn_ref[...], c_ref[...].reshape(TOK, width), TN).astype(BF16)
-    gk_ref[...] = gkv_ref[:VCOLS, :]
-
-
-def weight_grads(normed, cotangent, attn, d_query, grad_kv):
-    steps = 8
-    width, kv_width = D // steps, 2048 // steps
+def weight_kernel(nt_ref, c_ref, at_ref, dq_ref, gkv_ref, gx_ref, gg_ref, gi_ref, *outs):
+    gq_out, go_out, gk_out, gx_out, gg_out, gi_out = outs
+    gq_out[...] = dot(nt_ref[...], dq_ref[...]).astype(BF16)
+    go_out[...] = dot(at_ref[...], c_ref[...].reshape(TOK, c_ref.shape[-1])).astype(BF16)
+    gk_out[...] = gkv_ref[:VCOLS, :]
+    gx_out[...] = gx_ref[...]
+    gg_out[...] = gg_ref[...]
+    gi_out[...] = gi_ref[...]
+
+
+def weight_grads(normed_t, cotangent, attn_t, d_query, grad_kv, grad_x, grad_g, grad_image):
+    steps = 4
+    width, kv_width, im_width = D // steps, 2048 // steps, 32 * VCOLS // steps
     shape = jax.ShapeDtypeStruct
-    wide = pl.BlockSpec((4, 4, 16, width), lambda i: (0, 0, 0, i))
     whole = pl.BlockSpec((TOK, 256), lambda i: (0, 0))
+
+    def by_column(rows, cols):
+        return pl.BlockSpec((rows, cols), lambda i: (0, i))
+
     return pl.pallas_call(
         weight_kernel,
         grid=(steps,),
@@ -581,34 +633,42 @@
             shape((D, 256), BF16),
             shape((256, D), BF16),
             shape((VCOLS, 2048), BF16),
+            shape((8, D), BF16),
+            shape((1, D), F32),
+            shape((4, 32 * VCOLS), F32),
         ),
-        in_specs=[wide, wide, whole, whole, pl.BlockSpec((256, kv_width), lambda i: (0, i))],
+        in_specs=[
+            pl.BlockSpec((width, 256), lambda i: (i, 0)),
+            pl.BlockSpec((4, 4, 16, width), lambda i: (0, 0, 0, i)),
+            whole,
+            whole,
+            by_column(256, kv_width),
+            by_column(8, width),
+            by_column(1, width),
+            by_column(4, im_width),
+        ],
         out_specs=(
             pl.BlockSpec((width, 256), lambda i: (i, 0)),
-            pl.BlockSpec((256, width), lambda i: (0, i)),
-            pl.BlockSpec((VCOLS, kv_width), lambda i: (0, i)),
+            by_column(256, width),
+            by_column(VCOLS, kv_width),
+            by_column(8, width),
+            by_column(1, width),
+            by_column(4, im_width),
         ),
         compiler_params=pltpu.CompilerParams(vmem_limit_bytes=62 * 1024 * 1024),
         name="weight_grads",
-    )(normed, cotangent, attn, d_query, grad_kv)
+    )(normed_t, cotangent, attn_t, d_query, grad_kv, grad_x, grad_g, grad_image)
 
 
 def per_device(tokens, upstream, norm_gain, w_query, w_output, w_keyvalue, image_feats, visible):
     units = image_feats.astype(F32).reshape(4, 32, VCOLS)
     units = jnp.pad(units, ((0, 0), (0, 0), (0, 256 - VCOLS))).reshape(4, 32, 2, HD)
     units = units.transpose(1, 2, 0, 3).reshape(4, 2, 4, 8, HD)
-    normed, cotangent, attn, d_query, grad_kv, grad_x, grad_g, grad_image = run_layer(
+    results = run_layer(
         tokens[0], upstream[0], norm_gain, visible, units, w_query[0], w_output[0], w_keyvalue[0]
     )
-    grad_q, grad_out, grad_kv = weight_grads(normed, cotangent, attn, d_query, grad_kv)
-    return (
-        grad_x[None],
-        grad_g.reshape(1, D),
-        grad_q[None],
-        grad_out[None],
-        grad_kv[None],
-        grad_image,
-    )
+    grad_q, grad_out, grad_kv, grad_x, grad_g, grad_image = weight_grads(*results)
+    return (grad_x[None], grad_g, grad_q[None], grad_out[None], grad_kv[None], grad_image)
 
 
 def solution(mesh):

time: 168 us -> 152 us (0.905)
  Pallas kernels: 162 us -> 150 us
  local copies, waits for them, and re-layouts: 4.51 us -> 1.79 us
    pallas_call x1, Pallas kernels: 151 us -> 141 us  [run_layer(): pl.pallas_call(layer_kernel, out_shape=(shape((D, 256), BF16), shape((4,...]
    unnamed x7 -> x0, local copies, waits for them, and re-layouts: 2.72 us -> none
    pallas_call x1, Pallas kernels: 11.2 us -> 9.06 us  [weight_grads(): pl.pallas_call(weight_kernel, grid=(steps,), out_shape=(shape((D, 256), B...]
where the time goes in v4:
time: 152 us
  Pallas kernels  150 us (99%)
  local copies, waits for them, and re-layouts  1.79 us (1%)
    pallas_call x1, Pallas kernels, run_layer(): pl.pallas_call(layer_kernel, out_shape=(shape((D, 256), BF16), shape((4,...  141 us
    pallas_call x1, Pallas kernels, weight_grads(): pl.pallas_call(weight_kernel, grid=(steps,), out_shape=(shape((D, 256), B...  9.06 us

profile of v4, /device:TPU:0, one launch (start us, length us, event | category | flops | bytes accessed | tf_op | source)
XLA Modules:
  0.0 152.2 jit_solution(6338385648668461677)
XLA Ops:
  0.6 1.0 reshape.25
  1.6 0.1 reshape.33
  1.7 0.7 copy.14
  2.5 140.7 %layer.1 = (bf16[8192,256]{1,0:T(8,128)(2,1)}, bf16[4,4,16,8192]{3,2,1,0:T(8,128)(2,1)}, bf16[256,256]{1,0:T(8,128)(2,1)}, bf16[256,256]{1,0:T(8,128)(2,1)}, bf1...) custom-call(bf16[8,8192]{1,0:T(8,128)(2,1)} %bitcast.19, ...), custom_call_target="tpu_custom_call" | custom-call | flops 6000000000 | bytes 20971520 | tf_op jit(solution)/shard_map/layer/pallas_call | solution.py:561
  143.2 9.1 %weight_grads.1 = (bf16[8192,256]{1,0:T(8,128)(2,1)}, bf16[256,8192]{1,0:T(8,128)(2,1)}, bf16[240,2048]{1,0:T(8,128)(2,1)}, bf16[8,8192]{1,0:T(8,128)(2,1)}, f32[1,8192]{1,0:T(1,128)}, /*index=5*/f32[4,7680]{1,0:T(4,128)}) custom-call(bf16[8192,256]{1,0:T(8,128)(2,1)} %get-tuple-element.20.nt_ref, bf16[4,4,16,8192]{3,2,1,0:T(8,128)(2,1)} %get-tuple-element.21.c_ref, ...), custom_call_target="tpu_custom_call" | custom-call | tf_op jit(solution)/shard_map/weight_grads/pallas_call | solution.py:629
  (1 shorter events, 0.0 us)

commit v5 on v4

--- a/solution.py
+++ b/solution.py
@@ -126,10 +126,11 @@
 
 
 def layer_kernel(
-    tok_ref, cot_ref, gain_ref, vis_ref, unit_ref, wq_hbm, wo_hbm, wkv_hbm,
-    n_out, c_out, attn_out, dq_out, gkv_out, gx_out, gg_out, gi_out,
+    tok_ref, cot_ref, gain_ref, vis_ref, feat_ref, wq_hbm, wo_hbm, wkv_hbm,
+    n_out, c_out, attn_hbm, dq_hbm, gkv_hbm, gx_out, gg_out, gi_out,
+    attn_out, dq_out, gkv_out,
     n_all, c_all, n_t, wq, wo, wkv,
-    u_y, u_z, u_x, feat_all,
+    unit_ref, u_y, u_z, u_x, feat_all,
     fold_n, fold_c, from_n, from_c,
     feat_t, pk, pv, kx, ks0, ks1, ks2, ks3, v_y, v_z, vs1, vs2, vs3, vx, keys, values,
     dk, dv, rk, rv, dkg, dvg,
@@ -161,6 +162,12 @@
         pl.loop(0, HALF // CHUNK)(step)
 
     fold_step(normed_at, fold_n)
+
+    wide = feat_ref[...].astype(F32)
+    for m in range(32):
+        cols = wide[:, m * VCOLS : (m + 1) * VCOLS]
+        rest = jnp.concatenate([cols[:, HD:], jnp.zeros((4, 256 - VCOLS), F32)], axis=1)
+        unit_ref[m // 8, (m // 4) % 2, m % 4] = jnp.concatenate([cols[:, :HD], rest], axis=0)
     ready()
     x_n = net.send("x", 1, fold_n, from_n)
     u_y[y] = unit_ref[:, :, y]
@@ -260,6 +267,17 @@
         )
     for half in gather_c:
         half.middle()
+    for half in gather_n:
+        half.end()
+    loads[1].wait()
+
+    def query_step(i, acc):
+        cols = pl.ds(pl.multiple_of(i * CHUNK, CHUNK), CHUNK)
+        return acc + dot(n_all[:, :, :, cols].reshape(TOK, CHUNK), wq[cols, :])
+
+    query = lax.fori_loop(0, D // CHUNK, query_step, jnp.zeros((TOK, 256), F32)).astype(BF16)
+    for half in gather_c:
+        half.spread()
     k_2 = []
     for n, rows in enumerate(halves):
         k_x[n].wait_recv()
@@ -278,8 +296,6 @@
                 total += vs2[n, d, b]
             vs3[n, b] = total
         v_x.append(net.send("x", 1, vs3.at[n, 1 - x], vx.at[n]))
-    for half in gather_c:
-        half.spread()
     k_3 = []
     for n in range(2):
         arrive(k_2[n])
@@ -291,6 +307,8 @@
         k_3.append(
             net.ring(axes[n][1], lambda d: along(n, 1, ks2.at[n], d), lambda d: ks3.at[n, d - 1])
         )
+    for half in gather_c:
+        half.forward()
     for n in range(2):
         v_x[n].wait_recv()
         values[y, 64 * n : 64 * n + 64] = (vs3[n, x] + vx[n]).astype(BF16)
@@ -303,18 +321,6 @@
         keys[y, 64 * n : 64 * n + 64] = total.astype(BF16)
     k_3 = net.ring("y", lambda d: keys.at[y], lambda d: keys.at[y])
 
-    for half in gather_n:
-        half.end()
-    loads[1].wait()
-
-    def query_step(i, acc):
-        cols = pl.ds(pl.multiple_of(i * CHUNK, CHUNK), CHUNK)
-        return acc + dot(n_all[:, :, :, cols].reshape(TOK, CHUNK), wq[cols, :])
-
-    query = lax.fori_loop(0, D // CHUNK, query_step, jnp.zeros((TOK, 256), F32)).astype(BF16)
-
-    for half in gather_c:
-        half.forward()
     stores = []
     arrive(k_3)
     arrive(v_3)
@@ -357,6 +363,10 @@
         dq_out[:, heads] = dot(d_score, key).astype(BF16)
         d_key += dot(d_score, query[:, heads], TN)
         d_value += dot(weights[j], da, TN)
+    for i, (src, dst) in enumerate(((attn_out, attn_hbm), (dq_out, dq_hbm))):
+        copy = pltpu.make_async_copy(src, dst, local_sems.at[5 + i])
+        copy.start()
+        stores.append(copy)
     dk[...] = d_key.astype(BF16).reshape(4, 128, HD)
     dv[...] = d_value.astype(BF16).reshape(4, 128, HD)
     dk_1 = net.ring("y", lambda d: dk.at[net.coord("y", d)], lambda d: rk.at[d - 1])
@@ -497,6 +507,9 @@
     for h in range(8):
         for at, full in ((h * HD, dkg), (1024 + h * HD, dvg)):
             gkv_out[:, at : at + HD] = dot(feat_t[...], full[h // 2, h % 2].reshape(512, HD)).astype(BF16)
+    copy = pltpu.make_async_copy(gkv_out, gkv_hbm, local_sems.at[7])
+    copy.start()
+    stores.append(copy)
     arrive(g_2)
     gx2[x] = (gy[0] + gy[1]) + (gy[2] + gy[3])
     g_3 = net.send("x", 1, gx2.at[x], gx2.at[x])
@@ -552,7 +565,7 @@
     net.finish()
 
 
-def run_layer(tokens, cotangent, gain_row, visible, units, w_q, w_o, w_kv):
+def run_layer(tokens, cotangent, gain_row, visible, feats, w_q, w_o, w_kv):
     any_spec = pl.BlockSpec(memory_space=pl.ANY)
     vmem = pl.BlockSpec(memory_space=pltpu.VMEM)
     smem = pl.BlockSpec(memory_space=pltpu.SMEM)
@@ -571,10 +584,11 @@
             shape((4, 32 * VCOLS), F32),
         ),
         in_specs=[vmem, vmem, vmem, smem, vmem, any_spec, any_spec, any_spec],
-        out_specs=(any_spec, any_spec, vmem, vmem, vmem, vmem, vmem, vmem),
+        out_specs=(any_spec,) * 5 + (vmem,) * 3,
         scratch_shapes=[
+            b(256, TOK), b(TOK, 256), b(256, 2048),
             b(4, 4, 16, D), b(4, 4, 16, D), b(D, 256), b(D, 256), b(256, D), b(256, 2048),
-            f(4, 4, 2, 8, HD), f(4, 4, 2, 8, HD), f(2, 4, 4, 8, HD), b(4, 128, 256),
+            f(4, 2, 4, 8, HD), f(4, 4, 2, 8, HD), f(4, 4, 2, 8, HD), f(2, 4, 4, 8, HD), b(4, 128, 256),
             b(16, HALF), b(16, HALF), b(16, HALF), b(16, HALF),
             b(256, 512), f(4, 2, 4, 128, HD), b(4, 2, 4, 128, HD),
             f(2, 4, 4, 64, HD), f(2, 4, 4, 64, HD), f(2, 3, 4, 64, HD),
@@ -595,7 +609,7 @@
             f(1, D), f(4, 8, 1024), f(4, 8, 1024), f(2, 8, 1024),
             pltpu.SemaphoreType.DMA((NSEM,)),
             pltpu.SemaphoreType.DMA((NSEM,)),
-            pltpu.SemaphoreType.DMA((5,)),
+            pltpu.SemaphoreType.DMA((8,)),
         ],
         compiler_params=pltpu.CompilerParams(
             collective_id=0, has_side_effects=True, vmem_limit_bytes=58 * 1024 * 1024
@@ -604,7 +618,7 @@
             flops=6 * 10**9, bytes_accessed=20 * 2**20, transcendentals=2 * 256 * 512
         ),
         name="layer",
-    )(tokens, cotangent, gain_row, visible, units, w_q, w_o, w_kv)
+    )(tokens, cotangent, gain_row, visible, feats, w_q, w_o, w_kv)
 
 
 def weight_kernel(nt_ref, c_ref, at_ref, dq_ref, gkv_ref, gx_ref, gg_ref, gi_ref, *outs):
@@ -618,8 +632,8 @@
 
 
 def weight_grads(normed_t, cotangent, attn_t, d_query, grad_kv, grad_x, grad_g, grad_image):
-    steps = 4
-    width, kv_width, im_width = D // steps, 2048 // steps, 32 * VCOLS // steps
+    steps = 2
+    width, kv_width = D // steps, 2048 // steps
     shape = jax.ShapeDtypeStruct
     whole = pl.BlockSpec((TOK, 256), lambda i: (0, 0))
 
@@ -645,7 +659,7 @@
             by_column(256, kv_width),
             by_column(8, width),
             by_column(1, width),
-            by_column(4, im_width),
+            pl.BlockSpec((4, 32 * VCOLS), lambda i: (0, 0)),
         ],
         out_specs=(
             pl.BlockSpec((width, 256), lambda i: (i, 0)),
@@ -653,7 +667,7 @@
             by_column(VCOLS, kv_width),
             by_column(8, width),
             by_column(1, width),
-            by_column(4, im_width),
+            pl.BlockSpec((4, 32 * VCOLS), lambda i: (0, 0)),
         ),
         compiler_params=pltpu.CompilerParams(vmem_limit_bytes=62 * 1024 * 1024),
         name="weight_grads",
@@ -661,11 +675,8 @@
 
 
 def per_device(tokens, upstream, norm_gain, w_query, w_output, w_keyvalue, image_feats, visible):
-    units = image_feats.astype(F32).reshape(4, 32, VCOLS)
-    units = jnp.pad(units, ((0, 0), (0, 0), (0, 256 - VCOLS))).reshape(4, 32, 2, HD)
-    units = units.transpose(1, 2, 0, 3).reshape(4, 2, 4, 8, HD)
     results = run_layer(
-        tokens[0], upstream[0], norm_gain, visible, units, w_query[0], w_output[0], w_keyvalue[0]
+        tokens[0], upstream[0], norm_gain, visible, image_feats, w_query[0], w_output[0], w_keyvalue[0]
     )
     grad_q, grad_out, grad_kv, grad_x, grad_g, grad_image = weight_grads(*results)
     return (grad_x[None], grad_g, grad_q[None], grad_out[None], grad_kv[None], grad_image)

time: 152 us -> 148 us (0.974)
  Pallas kernels: 150 us -> 147 us
  local copies, waits for them, and re-layouts: 1.79 us -> 0 us
    reshape x3 -> x0, local copies, waits for them, and re-layouts: 1.79 us -> none  [the longest x1 0.98 us: per_device(): units = image_feats.astype(F32).reshape(4, 32, VCOLS)]
    pallas_call x1, Pallas kernels: 141 us -> 139 us  [run_layer(): pl.pallas_call(layer_kernel, out_shape=(shape((D, 256), BF16), shape((4,...]
where the time goes in v5:
time: 148 us
  Pallas kernels  147 us (99%)
    pallas_call x1, Pallas kernels, run_layer(): pl.pallas_call(layer_kernel, out_shape=(shape((D, 256), BF16), shape((4,...  139 us
    pallas_call x1, Pallas kernels, weight_grads(): pl.pallas_call(weight_kernel, grid=(steps,), out_shape=(shape((D, 256), B...  7.97 us

profile of v5, /device:TPU:0, one launch (start us, length us, event | category | flops | bytes accessed | tf_op | source)
XLA Modules:
  0.0 147.6 jit_solution(6537811056623925354)
XLA Ops:
  0.6 139.0 %layer.1 = (bf16[8192,256]{1,0:T(8,128)(2,1)}, bf16[4,4,16,8192]{3,2,1,0:T(8,128)(2,1)}, bf16[256,256]{1,0:T(8,128)(2,1)}, bf16[256,256]{1,0:T(8,128)(2,1)}, bf1...) custom-call(bf16[8,8192]{1,0:T(8,128)(2,1)} %bitcast.15, ...), custom_call_target="tpu_custom_call" | custom-call | flops 6000000000 | bytes 20971520 | tf_op jit(solution)/shard_map/layer/pallas_call | solution.py:574
  139.6 8.0 %weight_grads.1 = (bf16[8192,256]{1,0:T(8,128)(2,1)}, bf16[256,8192]{1,0:T(8,128)(2,1)}, bf16[240,2048]{1,0:T(8,128)(2,1)}, bf16[8,8192]{1,0:T(8,128)(2,1)}, f32[1,8192]{1,0:T(1,128)}, /*index=5*/f32[4,7680]{1,0:T(4,128)}) custom-call(bf16[8192,256]{1,0:T(8,128)(2,1)} %get-tuple-element.20.nt_ref, bf16[4,4,16,8192]{3,2,1,0:T(8,128)(2,1)} %get-tuple-element.21.c_ref, ...), custom_call_target="tpu_custom_call" | custom-call | tf_op jit(solution)/shard_map/weight_grads/pallas_call | solution.py:643

commit v6 on v5

--- a/solution.py
+++ b/solution.py
@@ -431,6 +431,10 @@
     da_far = reduce_far("y", 0, via_a)
     columns(HALF, D, d_normed_step)
     db_far = reduce_far("z", HALF, via_b)
+    columns(0, D, gain_step)
+    for i in range(8):
+        gz[z, i : i + 1, :] = gain_part[:, i * 1024 : (i + 1) * 1024]
+    g_1 = net.ring("z", lambda d: gz.at[z], lambda d: gz.at[z])
     arrive(dk_1)
     arrive(dv_1)
     total = dk[y].astype(F32)
@@ -451,11 +455,6 @@
     dv_2.wait_recv()
     for part in gather_d:
         part.start()
-    columns(0, D, gain_step)
-    for i in range(8):
-        gz[z, i : i + 1, :] = gain_part[:, i * 1024 : (i + 1) * 1024]
-    g_1 = net.ring("z", lambda d: gz.at[z], lambda d: gz.at[z])
-
     for part in gather_d:
         part.middle()
     da_near = reduce_on("y", 0, via_a, relay_a, near_a, da_far)

time: 148 us -> 148 us (level)
  no operation moved by 1% of the time
where the time goes in v6:
time: 148 us
  Pallas kernels  147 us (99%)
    pallas_call x1, Pallas kernels, run_layer(): pl.pallas_call(layer_kernel, out_shape=(shape((D, 256), BF16), shape((4,...  139 us
    pallas_call x1, Pallas kernels, weight_grads(): pl.pallas_call(weight_kernel, grid=(steps,), out_shape=(shape((D, 256), B...  7.97 us

profile of v6, /device:TPU:0, one launch (start us, length us, event | category | flops | bytes accessed | tf_op | source)
XLA Modules:
  0.0 147.6 jit_solution(1451356788660406532)
XLA Ops:
  0.6 139.0 %layer.1 = (bf16[8192,256]{1,0:T(8,128)(2,1)}, bf16[4,4,16,8192]{3,2,1,0:T(8,128)(2,1)}, bf16[256,256]{1,0:T(8,128)(2,1)}, bf16[256,256]{1,0:T(8,128)(2,1)}, bf1...) custom-call(bf16[8,8192]{1,0:T(8,128)(2,1)} %bitcast.15, ...), custom_call_target="tpu_custom_call" | custom-call | flops 6000000000 | bytes 20971520 | tf_op jit(solution)/shard_map/layer/pallas_call | solution.py:573
  139.6 8.0 %weight_grads.1 = (bf16[8192,256]{1,0:T(8,128)(2,1)}, bf16[256,8192]{1,0:T(8,128)(2,1)}, bf16[240,2048]{1,0:T(8,128)(2,1)}, bf16[8,8192]{1,0:T(8,128)(2,1)}, f32[1,8192]{1,0:T(1,128)}, /*index=5*/f32[4,7680]{1,0:T(4,128)}) custom-call(bf16[8192,256]{1,0:T(8,128)(2,1)} %get-tuple-element.20.nt_ref, bf16[4,4,16,8192]{3,2,1,0:T(8,128)(2,1)} %get-tuple-element.21.c_ref, ...), custom_call_target="tpu_custom_call" | custom-call | tf_op jit(solution)/shard_map/weight_grads/pallas_call | solution.py:642
